TPU v7x, 32 devices: a whole 2x2x4 slice. The times are simulated.
32 devices in a mesh: rep: 16 (over z, y, core), shard: 2 (over x).
Axes of the slice: x: 2, y: 2, z: 4, core: 2. Of those that a mesh axis runs over, the one named last changes fastest.
Arguments:
- hidden_in: bfloat16 [4096, 896], P(('rep', 'shard')), may hold values from -6 to 6
- segments: int32 [4096], P(('rep', 'shard')), may hold values from 0 to 15, never falling along the last dimension, each value on 1 to 512 neighbouring positions
- attn_gain: bfloat16 [896], P('shard'), may hold values from 0.5 to 1.5
- w_query: bfloat16 [896, 896], P('shard'), may hold values from -0.1875 to 0.1875
- b_query: bfloat16 [896], P('shard'), may hold values from -3 to 3
- w_key: bfloat16 [896, 128], P('shard'), may hold values from -0.1875 to 0.1875
- b_key: bfloat16 [128], P('shard'), may hold values from -3 to 3
- w_value: bfloat16 [896, 128], P('shard'), may hold values from -0.1875 to 0.1875
- b_value: bfloat16 [128], P('shard'), may hold values from -3 to 3
- w_out: bfloat16 [896, 896], P('shard'), may hold values from -0.75 to 0.75
- mlp_gain: bfloat16 [896], P('shard'), may hold values from 0.5 to 1.5
- w_gate: bfloat16 [896, 4864], P('shard'), may hold values from -0.1875 to 0.1875
- w_up: bfloat16 [896, 4864], P('shard'), may hold values from -0.1875 to 0.1875
- w_down: bfloat16 [4864, 896], P('shard'), may hold values from -0.078125 to 0.078125
- cotangent: bfloat16 [4096, 896], P(('rep', 'shard')), may hold values from -6 to 6
Outputs:
- layer_out: float32 [4096, 896], P(('rep', 'shard'))
- grad_input: float32 [4096, 896], P(('rep', 'shard'))
- grad_attn_gain: float32 [896], P('shard')
- grad_w_query: float32 [896, 896], P('shard')
- grad_b_query: float32 [896], P('shard')
- grad_w_key: float32 [896, 128], P('shard')
- grad_b_key: float32 [128], P('shard')
- grad_w_value: float32 [896, 128], P('shard')
- grad_b_value: float32 [128], P('shard')
- grad_w_out: float32 [896, 896], P('shard')
- grad_mlp_gain: float32 [896], P('shard')
- grad_w_gate: float32 [896, 4864], P('shard')
- grad_w_up: float32 [896, 4864], P('shard')
- grad_w_down: float32 [4864, 896], P('shard')
Inputs may be any that keep to these rules, and one draw needn't show every extreme that they name: `segments`: segment numbers never fall along the tokens; each segment holds 1 to 512 tokens and one holds exactly 512.
All inputs are finite; a program needn't handle non-finite values.
Results may differ from a plain program's by a relative error of at most 0.019.
The roundings to bfloat16 on the way count: a program that leaves them out, or rounds other values in their place, can miss the bound.
Values may be sent and summed in bfloat16 or wider, within the bound.
No kernel may reach another device: no remote copies, remote signals or barrier semaphores. Data moves between devices by JAX's collectives and lax.ppermute only.
A program may use at most 192 MiB of HBM per device.

v0:
```python
import math

import jax
import jax.numpy as jnp
from jax import lax
from jax.experimental import pallas as pl
from jax.experimental.pallas import tpu as pltpu
from jax.sharding import PartitionSpec as P

D = 896
HEADS = 14
KV_HEADS = 2
HEAD_DIM = 64
SEQ = 512


EPSILON = 1e-06
ROPE_THETA = 1000000.0
MASKED = -1e30

CORES = 2
ALONG_Z = 4


def passed_along(shard, axis, by):
    peers = lax.axis_size(axis)
    pairs = [(i, i + by) for i in range(peers) if 0 <= i + by < peers]
    return lax.ppermute(shard, axis, pairs)


def rep_sizes():
    planes = lax.axis_size("rep") // CORES
    zs = min(ALONG_Z, planes)
    return (zs, planes // zs)


def own_place():
    zs, ys = rep_sizes()
    rep = lax.axis_index("rep")
    plane = rep // CORES
    return {"z": plane // ys, "y": plane % ys, "core": rep % CORES, "shard": lax.axis_index("shard")}


def steps_of(axis):
    zs, ys = rep_sizes()
    size = {"z": zs, "y": ys, "core": CORES, "shard": lax.axis_size("shard")}[axis]
    return [(axis, 1 << i) for i in range(size.bit_length() - 1)]


def swap(value, step):
    axis, bit = step
    if axis == "shard":
        peers = lax.axis_size("shard")
        return lax.ppermute(value, "shard", [(i, i ^ bit) for i in range(peers)])
    zs, ys = rep_sizes()
    pairs = []
    for rep in range(zs * ys * CORES):
        at = {"z": rep // CORES // ys, "y": rep // CORES % ys, "core": rep % CORES}
        at[axis] ^= bit
        pairs.append((rep, (at["z"] * ys + at["y"]) * CORES + at["core"]))
    return lax.ppermute(value, "rep", pairs)


def own_bit(place, step):
    return place[step[0]] // step[1] % 2


def nothing(*refs):
    pass


def after(value, *earlier):
    anywhere = pl.BlockSpec(memory_space=pl.ANY)
    return pl.pallas_call(
        nothing,
        out_shape=jax.ShapeDtypeStruct(value.shape, value.dtype),
        in_specs=[anywhere] * (1 + len(earlier)),
        out_specs=anywhere,
        input_output_aliases={0: 0},
        cost_estimate=pl.CostEstimate(flops=0, bytes_accessed=0, transcendentals=0),
        name="after",
    )(value, *earlier)


def pick(whole, at, axis=0):
    return lax.dynamic_index_in_dim(whole, at, axis, keepdims=False)


def ordered(mine, got, place, step, axis=0):
    first = own_bit(place, step) == 0
    return jnp.where(
        first, jnp.concatenate([mine, got], axis=axis), jnp.concatenate([got, mine], axis=axis)
    )


def gather(piece, place, steps):
    for step in steps:
        piece = ordered(piece, swap(piece, step), place, step)
    return piece


def scatter_step(parts, place, step, axis=0, earlier=()):
    at = own_bit(place, step)
    got = swap(pick(parts, 1 - at, axis), step)
    if earlier:
        got = after(got, *earlier)
    total = pick(parts, at, axis).astype(jnp.float32) + got.astype(jnp.float32)
    return total.astype(jnp.bfloat16)


def scatter(parts, place, steps, lead=0, earlier=()):
    for index, step in enumerate(steps):
        parts = scatter_step(
            parts, place, step, lead + len(steps) - 1 - index, earlier[index : index + 1]
        )
    return parts


def exchange(parts, place, earlier):
    shards = lax.axis_size("shard")
    if shards == 2:
        at = place["shard"]
        got = after(swap(pick(parts, 1 - at), ("shard", 1)), earlier)
        return ordered(pick(parts, at)[None], got[None], place, ("shard", 1))
    return lax.all_to_all(parts, "shard", split_axis=0, concat_axis=0, tiled=True)


def group_tokens(rows, steps):
    for step in steps:
        rows = jnp.concatenate([rows, swap(rows, step)], axis=0)
    return rows


def group_step(parts, step, earlier=()):
    half = parts.shape[0] // 2
    sent = parts[half:]
    if step[0] != "core":
        sent = sent.astype(jnp.bfloat16)
    got = swap(sent, step)
    if earlier:
        got = after(got, *earlier)
    return parts[:half] + got.astype(jnp.float32)


def group_sum(parts, steps):
    for step in steps[::-1]:
        parts = group_step(parts, step)
    return parts


def rope_tables(positions):
    half_width = HEAD_DIM // 2
    inverse = ROPE_THETA ** (-(jnp.arange(half_width, dtype=jnp.float32) * 2.0) / HEAD_DIM)
    angle_half = positions.astype(jnp.float32)[:, None] * inverse[None, :]
    angle_full = jnp.concatenate([angle_half, angle_half], axis=-1)
    return (jnp.cos(angle_full), jnp.sin(angle_full))


def rotate_half(values):
    half_width = values.shape[-1] // 2
    return jnp.concatenate([-values[..., half_width:], values[..., :half_width]], axis=-1)


def rotate_back(values):
    half_width = values.shape[-1] // 2
    return jnp.concatenate([values[..., half_width:], -values[..., :half_width]], axis=-1)


def apply_rope(values, cosine, sine_table):
    return values * cosine[:, None, :] + rotate_half(values) * sine_table[:, None, :]


def undo_rope(grads, cosine, sine_table):
    return grads * cosine[:, None, :] + rotate_back(grads * sine_table[:, None, :])


def rms_forward(values, gain):
    inv_scale = lax.rsqrt(jnp.mean(values * values, axis=-1, keepdims=True) + EPSILON)
    normed = values * inv_scale
    return (normed, inv_scale, normed * gain)


def rms_backward(grads, normed, inv_scale, gain):
    through = grads * gain
    inner = jnp.mean(through * normed, axis=-1, keepdims=True)
    return (inv_scale * (through - normed * inner), jnp.sum(grads * normed, axis=0))


def spans(first, count, size):
    cuts = []
    at = first
    while at < first + count:
        end = min((at // size + 1) * size, first + count)
        cuts.append((at // size, at % size, at - first, end - at))
        at = end
    return cuts


def kept_of(index, ff_block, ff_own):
    at = min(index * ff_block, ff_own - ff_block)
    return (at, min(index * ff_block - at, ff_block))


def weight_sums(mlp_rows, cot_rows, hidden_low, grad_gate, grad_up, zs, shards):
    tokens, width = mlp_rows.shape
    units = hidden_low.shape[1]
    rows = width // zs
    d_z = width // shards // zs
    f_z = units // zs

    def kernel(x_ref, cot_ref, hidden_ref, gate_ref, up_ref, out_ref):
        def chunks(size):
            return [(at, min(256, size - at)) for at in range(0, size, 256)]

        def column_sum(left, right_ref):
            got = jnp.dot(left, right_ref[...], preferred_element_type=jnp.float32)
            return got.astype(jnp.bfloat16)

        for first, wide in chunks(units):
            got = column_sum(hidden_ref[:, first : first + wide].T, cot_ref)
            for z, row, at, count in spans(first, wide, f_z):
                for tile in range(width // 128):
                    piece = got[at : at + count, tile * 128 : (tile + 1) * 128]
                    for to, to_row, from_row, length in spans(tile * f_z + row, count, rows):
                        out_ref[z, 0, to_row : to_row + length, to * 128 : (to + 1) * 128] = piece[
                            from_row : from_row + length
                        ]
        for first, wide in chunks(width):
            left = x_ref[:, first : first + wide].T
            for index, right_ref in ((1, gate_ref), (2, up_ref)):
                got = column_sum(left, right_ref)
                for part, row, at, count in spans(first, wide, d_z):
                    to_row = part // zs * d_z + row
                    out_ref[part % zs, index, to_row : to_row + count] = got[at : at + count]

    operands = (mlp_rows, cot_rows, hidden_low, grad_gate, grad_up)
    return pl.pallas_call(
        kernel,
        out_shape=jax.ShapeDtypeStruct((zs, 3, rows, units), jnp.bfloat16),
        in_specs=[pl.BlockSpec(memory_space=pltpu.VMEM)] * 5,
        out_specs=pl.BlockSpec(memory_space=pltpu.VMEM),
        compiler_params=pltpu.CompilerParams(vmem_limit_bytes=48 * 1024 * 1024),
        cost_estimate=pl.CostEstimate(
            flops=6 * tokens * width * units, bytes_accessed=12 * 1024 * 1024, transcendentals=0
        ),
        name="weight_sums",
    )(*operands)


def weights_in_place(all_all, shards, ff_own):
    zs, blocks, _, rows, units = all_all.shape
    width = rows * zs
    d_z = rows // shards
    f_z = units // zs

    def kernel(all_ref, gate_ref, up_ref, down_ref, wide_ref, sems):
        z = pl.program_id(0)
        for index in range(blocks):
            for tile in range(width // 128):
                for part, row, at, count in spans(tile * f_z, f_z, rows):
                    wide_ref[index, at : at + count, tile * 128 : (tile + 1) * 128] = all_ref[
                        0, index, 0, row : row + count, part * 128 : (part + 1) * 128
                    ].astype(jnp.float32)

        def move(index, skip):
            at = kept_of(index, units, ff_own)[0]
            to = pl.multiple_of(at + z * f_z + skip, 8)
            return pltpu.make_async_copy(
                wide_ref.at[index, pl.ds(skip, f_z - skip)],
                down_ref.at[pl.ds(to, f_z - skip)],
                sems.at[index],
            )

        def each_move(act):
            for index in range(blocks):
                dropped = kept_of(index, units, ff_own)[1]
                for place in range(zs):
                    skip = min(max(dropped - place * f_z, 0), f_z)
                    if skip < f_z:

                        @pl.when(z == place)
                        def _(index=index, skip=skip):
                            act(move(index, skip))

        each_move(lambda copy: copy.start())
        for number, out_ref in ((1, gate_ref), (2, up_ref)):
            for owner in range(shards):
                for index in range(blocks):
                    at, skip = kept_of(index, units, ff_own)
                    if skip < units:
                        out_ref[:, owner * ff_own + at + skip : owner * ff_own + at + units] = all_ref[
                            0, index, number, owner * d_z : (owner + 1) * d_z, skip:
                        ].astype(jnp.float32)
        each_move(lambda copy: copy.wait())

    wide = jax.ShapeDtypeStruct((d_z * zs, shards * ff_own), jnp.float32)
    return pl.pallas_call(
        kernel,
        grid=(zs,),
        out_shape=(wide, wide, jax.ShapeDtypeStruct((ff_own, width), jnp.float32)),
        in_specs=[pl.BlockSpec((1, blocks, 3, rows, units), lambda z: (z, 0, 0, 0, 0))],
        out_specs=(
            pl.BlockSpec((d_z, shards * ff_own), lambda z: (z, 0)),
            pl.BlockSpec((d_z, shards * ff_own), lambda z: (z, 0)),
            pl.BlockSpec(memory_space=pl.ANY),
        ),
        scratch_shapes=[
            pltpu.VMEM((blocks, f_z, width), jnp.float32),
            pltpu.SemaphoreType.DMA((blocks,)),
        ],
        compiler_params=pltpu.CompilerParams(vmem_limit_bytes=48 * 1024 * 1024),
        cost_estimate=pl.CostEstimate(flops=0, bytes_accessed=44 * 1024 * 1024, transcendentals=0),
        name="weights_in_place",
    )(all_all)


def prior_rows(rows, back_reach):
    parts = []
    for distance in range(back_reach, 0, -1):
        parts.append(passed_along(rows, ("rep", "shard"), distance))
    parts.append(rows)
    return jnp.concatenate(parts, axis=0)


def return_rows(grads, tok_rows, back_reach):
    total = grads[back_reach * tok_rows :]
    for distance in range(back_reach, 0, -1):
        first_row = (back_reach - distance) * tok_rows
        total = total + passed_along(
            grads[first_row : first_row + tok_rows], ("rep", "shard"), -distance
        )
    return total


def token_sum(left, right):
    return lax.dot_general(
        left, right, (((0,), (0,)), ((), ())), preferred_element_type=jnp.float32
    ).astype(jnp.bfloat16)


def per_device(
    hidden_in,
    segments,
    attn_gain,
    w_query,
    b_query,
    w_key,
    b_key,
    w_value,
    b_value,
    w_out,
    mlp_gain,
    w_gate,
    w_up,
    w_down,
    cotangent,
):
    tok_rows = hidden_in.shape[0]
    back_reach = (SEQ - 2) // tok_rows + 1
    head_group = HEADS // KV_HEADS
    kv_width = KV_HEADS * HEAD_DIM
    qkv_width = D + 2 * kv_width
    scale = 1.0 / math.sqrt(HEAD_DIM)
    place = own_place()
    core, shard = place["core"], place["shard"]
    shards = lax.axis_size("shard")
    zs, ys = rep_sizes()
    d_own = D // shards
    shard_steps, y_steps, z_steps, core_steps = [
        steps_of(axis) for axis in ("shard", "y", "z", "core")
    ]
    group_steps = shard_steps + y_steps + core_steps

    ff_own = w_down.shape[0]
    blocks = ys * CORES
    ff_block = min(ff_own, -(-ff_own // (blocks * 128)) * 128)
    block = place["y"] * CORES + core
    block_at = jnp.minimum(block * ff_block, ff_own - ff_block)

    w_qkv = jnp.concatenate([w_query, w_key, w_value], axis=1)
    qkv_half = pick(w_qkv.reshape(CORES, d_own // CORES, qkv_width), core)
    small = jnp.concatenate([attn_gain, b_query, b_key, b_value, mlp_gain])
    own_segments = segments + 1
    group_is_reach = shards == 2 and CORES * shards == back_reach
    window_at = (core * shards + shard) * tok_rows

    def window(rows):
        rows = rows.reshape((2 * back_reach * tok_rows,) + rows.shape[4:])
        return lax.dynamic_slice_in_dim(rows, window_at, (back_reach + 1) * tok_rows, 0)

    def as_rows(vector, count):
        return jnp.pad(vector, (0, count * qkv_width - vector.shape[0])).reshape(count, qkv_width)

    def columns_of(weight, owner):
        return lax.dynamic_slice_in_dim(weight, owner * ff_own + block_at, ff_block, 1)

    columns_sent = [
        pick(
            columns_of(weight, (shard + 1) % shards).reshape(2, d_own // 2, ff_block),
            own_bit(place, z_steps[0]),
        )
        for weight in (w_gate, w_up)
    ]
    if group_is_reach:
        far = passed_along(own_segments, ("rep", "shard"), back_reach)
        both = jnp.concatenate([far, own_segments]).astype(jnp.bfloat16)
        extra = -(-(small.shape[0] + 2 * tok_rows) // (16 * qkv_width)) * 16
        sent = as_rows(jnp.concatenate([small, both]), extra)
        got = swap(jnp.concatenate([qkv_half, sent], axis=0), shard_steps[0])
        got = after(got, *columns_sent)
        got_qkv, got_small = got[:-extra], got[-extra:].reshape(-1)
        small_all = ordered(small[None], got_small[None, : small.shape[0]], place, shard_steps[0])
        got_both = got_small[small.shape[0] : small.shape[0] + 2 * tok_rows]
        both = ordered(
            both.reshape(2, 1, tok_rows), got_both.reshape(2, 1, tok_rows), place, shard_steps[0], 1
        )
        sent = as_rows(both.reshape(-1), 16)
        other_qkv = swap(jnp.concatenate([got_qkv, sent], axis=0), core_steps[0])
        got_both = other_qkv[-16:].reshape(-1)[: both.size].reshape(2, 1, shards, tok_rows)
        both = ordered(both[:, None], got_both, place, core_steps[0], 1)
        ext_segments = window(both.reshape(both.shape)).astype(jnp.int32)
        other_qkv = ordered(got_qkv, other_qkv[:-16], place, core_steps[0])
        full_qkv = ordered(w_qkv, other_qkv, place, shard_steps[0])
    else:
        small_all = gather(small[None], place, shard_steps)
        ext_segments = prior_rows(own_segments, back_reach)
        got_qkv = w_qkv
        full_qkv = lax.all_gather(w_qkv, "shard", axis=0, tiled=True)
    kv_own = kv_width // shards
    cuts = [0, d_own, 2 * d_own, 2 * d_own + kv_own, 2 * d_own + 2 * kv_own, small.shape[0]]
    gain_low, bias_query, bias_key, bias_value, mlp_low = [
        small_all[:, a:b].reshape(-1) for a, b in zip(cuts[:-1], cuts[1:])
    ]
    bias_qkv = jnp.concatenate([bias_query, bias_key, bias_value]).astype(jnp.float32)

    ext_len = ext_segments.shape[0]
    column = jnp.arange(ext_len, dtype=jnp.int32)
    row_at = back_reach * tok_rows + jnp.arange(tok_rows, dtype=jnp.int32)
    same_doc = own_segments[:, None] == ext_segments[None, :]
    doc_first = jnp.min(jnp.where(same_doc, column[None, :], ext_len), axis=1)
    positions = row_at - doc_first
    allowed = same_doc & (column[None, :] <= row_at[:, None])
    cosine, sine_table = rope_tables(positions)
    input_wide = hidden_in.astype(jnp.float32)
    gain_attn = gain_low.astype(jnp.float32)
    gain_mlp = mlp_low.astype(jnp.float32)
    normed_attn, inv_attn, scaled_attn = rms_forward(input_wide, gain_attn)
    attn_input = scaled_attn.astype(jnp.bfloat16)

    def all_rows(own, fetched):
        if shards == 2:
            for step in y_steps:
                fetched = ordered(fetched, swap(fetched, step), place, step)
            other = ordered(fetched, swap(fetched, core_steps[0]), place, core_steps[0])
            return ordered(own, other, place, shard_steps[0])
        return lax.all_gather(own, "shard", axis=0, tiled=True)


    def block_rows(weight, sent, earlier):
        own = columns_of(weight, shard)
        if shards == 2:
            got = swap(after(sent, earlier), shard_steps[0])
            other = ordered(got, swap(got, z_steps[0]), place, z_steps[0])
            return (ordered(own, other, place, shard_steps[0]), got, other)
        sent = jnp.stack([columns_of(weight, owner) for owner in range(shards)])
        got = lax.all_to_all(sent, "shard", split_axis=0, concat_axis=0, tiled=True)
        return (got.reshape(D, ff_block), got, got)

    out_part = pick(w_out.reshape(CORES, ys, d_own // CORES // ys, D), core)
    out_part = pick(out_part, place["y"])
    got_out = swap(after(out_part, got_qkv), shard_steps[0])
    cot_shards = group_tokens(after(cotangent, got_qkv), shard_steps)
    cot_ys = group_tokens(cot_shards, y_steps)
    cot_rows = group_tokens(cot_ys, core_steps)
    gate_here, got_gate, other_gate = block_rows(w_gate, columns_sent[0], got_qkv)
    up_here, got_up, other_up = block_rows(w_up, columns_sent[1], got_qkv)
    down_rows = lax.dynamic_slice_in_dim(w_down, block_at, ff_block, 0)
    once = block_at + jnp.arange(ff_block, dtype=jnp.int32) >= block * ff_block
    down_here = jnp.where(once[:, None], down_rows, jnp.zeros_like(down_rows))

    qkv_lin = jnp.dot(attn_input, full_qkv, preferred_element_type=jnp.float32) + bias_qkv
    rot = apply_rope(
        qkv_lin[:, : D + kv_width].reshape(tok_rows, HEADS + KV_HEADS, HEAD_DIM), cosine, sine_table
    ).astype(jnp.bfloat16)
    query_rot = rot[:, :HEADS]
    value_low = qkv_lin[:, D + kv_width :].astype(jnp.bfloat16)
    kv_own_rows = jnp.concatenate([rot[:, HEADS:].reshape(tok_rows, kv_width), value_low], axis=1)
    if group_is_reach:
        far = passed_along(kv_own_rows, ("rep", "shard"), back_reach)
        both = after(jnp.stack([far, kv_own_rows])[:, None], got_gate)
        both = ordered(both, swap(both, shard_steps[0]), place, shard_steps[0], 1)[:, None]
        both = ordered(both, swap(both, core_steps[0]), place, core_steps[0], 1)
        kv_ext = window(both)
    else:
        kv_ext = prior_rows(kv_own_rows, back_reach)
    full_out = all_rows(w_out, after(got_out, kv_own_rows))
    kv_ext = after(kv_ext, got_up, cot_shards)
    keys_ext = kv_ext[:, :kv_width].reshape(ext_len, KV_HEADS, HEAD_DIM)
    values_ext = kv_ext[:, kv_width:].reshape(ext_len, KV_HEADS, HEAD_DIM)
    queries = query_rot.reshape(tok_rows, KV_HEADS, head_group, HEAD_DIM)
    scores = (
        jnp.einsum("qkgd,wkd->kgqw", queries, keys_ext, preferred_element_type=jnp.float32) * scale
    )
    scores = jnp.where(allowed[None, None], scores, MASKED)
    row_max = jnp.max(scores, axis=-1, keepdims=True)
    raw_weights = jnp.exp(scores - row_max)
    row_total = jnp.sum(raw_weights, axis=-1, keepdims=True)
    probs_low = (raw_weights / row_total).astype(jnp.bfloat16)
    log_total = row_max + jnp.log(row_total)
    attn_rows = jnp.einsum(
        "kgqw,wkd->qkgd", probs_low, values_ext, preferred_element_type=jnp.float32
    ).astype(jnp.bfloat16)
    attn_out = attn_rows.reshape(tok_rows, D)
    after_attn = input_wide + jnp.dot(attn_out, full_out, preferred_element_type=jnp.float32)
    normed_mlp, inv_mlp, scaled_mlp = rms_forward(after_attn, gain_mlp)
    mlp_input = after(scaled_mlp.astype(jnp.bfloat16), other_gate, cot_ys)

    mlp_rows = group_tokens(mlp_input, shard_steps)
    mlp_rows = group_tokens(after(mlp_rows, other_up), y_steps + core_steps)
    gate_lin = jnp.dot(mlp_rows, gate_here, preferred_element_type=jnp.float32)
    up_lin = jnp.dot(mlp_rows, up_here, preferred_element_type=jnp.float32)
    gate_sig = jax.nn.sigmoid(gate_lin)
    gate_act = gate_lin * gate_sig
    hidden_low = (gate_act * up_lin).astype(jnp.bfloat16)
    z_halves = (2,) * len(z_steps)
    grad_hidden = jnp.einsum("td,fd->tf", cot_rows, down_here, preferred_element_type=jnp.float32)
    grad_gate_lin = (grad_hidden * up_lin * gate_sig * (1.0 + gate_lin * (1.0 - gate_sig))).astype(
        jnp.bfloat16
    )
    grad_up_lin = (grad_hidden * gate_act).astype(jnp.bfloat16)
    by_tiles = (d_own // zs) % 16 == 0 and (ff_block // zs) % 16 == 0 and ff_own % 128 == 0
    if by_tiles:
        all_parts = weight_sums(
            mlp_rows, cot_rows, hidden_low, grad_gate_lin, grad_up_lin, zs, shards
        )
    else:
        down_parts = token_sum(hidden_low, cot_rows)
        gate_parts = token_sum(mlp_rows, grad_gate_lin)
        up_parts = token_sum(mlp_rows, grad_up_lin)
    normed_parts = jnp.einsum(
        "tf,df->td", grad_gate_lin, gate_here, preferred_element_type=jnp.float32
    ) + jnp.einsum(
        "tf,df->td",
        grad_up_lin,
        up_here,
        preferred_element_type=jnp.float32,
    )
    block_rows_out = D // zs
    tiles_in, tiles_out = D // 128, ff_block // 128

    def as_block(parts):
        parts = parts.reshape(zs, ff_block // zs, tiles_in, 128).transpose(0, 2, 1, 3)
        parts = parts.reshape(zs, tiles_out, block_rows_out, 128).transpose(0, 2, 1, 3)
        return parts.reshape(zs, block_rows_out, ff_block)

    def from_block(whole):
        lead = whole.shape[:-2]
        whole = whole.reshape(lead + (block_rows_out, tiles_out, 128)).swapaxes(-3, -2)
        whole = whole.reshape(lead + (tiles_in, ff_block // zs, 128)).swapaxes(-3, -2)
        return whole.reshape(lead + (ff_block // zs, D))

    def by_z(parts):
        parts = parts.reshape(shards, zs, d_own // zs, ff_block).swapaxes(0, 1)
        return parts.reshape(zs, block_rows_out, ff_block)

    if not by_tiles:
        all_parts = jnp.stack([as_block(down_parts), by_z(gate_parts), by_z(up_parts)], axis=1)
    same_yc = [[z * blocks + index for z in range(zs)] for index in range(blocks)]
    all_sum = lax.psum_scatter(
        all_parts, "rep", scatter_dimension=0, axis_index_groups=same_yc, tiled=False
    )
    grad_mlp_normed = group_sum(normed_parts, group_steps)

    def from_rep(piece):
        whole = lax.all_gather(piece, "rep", axis=0)
        return whole.reshape((zs, blocks) + piece.shape)

    grad_part, grad_mlp_gain = rms_backward(grad_mlp_normed, normed_mlp, inv_mlp, gain_mlp)
    grad_after = cotangent.astype(jnp.float32) + grad_part
    after_low = grad_after.astype(jnp.bfloat16)
    out_parts = jnp.dot(
        after(hidden_low, after_low), down_here, preferred_element_type=jnp.float32
    )
    out_sums = group_sum(out_parts, y_steps + core_steps)

    def half_sum(left, right):
        columns = left.reshape(tok_rows, shards, CORES, d_own // CORES)
        kept, sent = pick(columns, core, 2), pick(columns, 1 - core, 2)
        columns = jnp.concatenate([kept, swap(sent, core_steps[0])], axis=0)
        right = jnp.concatenate([right, swap(right, core_steps[0])], axis=0)
        return token_sum(columns.reshape(CORES * tok_rows, -1), right)

    def shard_scatter(parts):
        parts = parts.reshape((shards, -1, parts.shape[1]))
        if shards == 2:
            return scatter(parts, place, shard_steps)
        return lax.psum_scatter(parts, "shard", scatter_dimension=0)

    out_sum = shard_scatter(half_sum(attn_out, after_low))
    grad_attn_out = jnp.einsum(
        "te,de->td", after_low, full_out, preferred_element_type=jnp.float32
    ).astype(jnp.bfloat16)
    grad_rows = grad_attn_out.reshape(tok_rows, KV_HEADS, head_group, HEAD_DIM)
    soft_probs = jnp.exp(scores - log_total)
    probs_back = soft_probs.astype(jnp.bfloat16)
    grad_values_ext = jnp.einsum(
        "kgqw,qkgd->wkd", probs_back, grad_rows, preferred_element_type=jnp.float32
    )
    grad_probs = jnp.einsum(
        "qkgd,wkd->kgqw", grad_rows, values_ext, preferred_element_type=jnp.float32
    )
    delta = jnp.sum(grad_rows.astype(jnp.float32) * attn_rows.astype(jnp.float32), axis=-1)
    delta = jnp.transpose(delta, (1, 2, 0))[..., None]
    grad_scores = (soft_probs * (grad_probs - delta) * scale).astype(jnp.bfloat16)
    grad_queries = jnp.einsum(
        "kgqw,wkd->qkgd", grad_scores, keys_ext, preferred_element_type=jnp.float32
    )
    grad_keys_ext = jnp.einsum(
        "kgqw,qkgd->wkd", grad_scores, queries, preferred_element_type=jnp.float32
    )
    grads_ext = jnp.concatenate(
        [grad_keys_ext.reshape(ext_len, kv_width), grad_values_ext.reshape(ext_len, kv_width)],
        axis=1,
    )
    grads_ext = after(grads_ext, out_sum, out_sums)
    layer_out = after_attn + group_sum(out_sums, shard_steps)
    grad_kv = return_rows(grads_ext, tok_rows, back_reach)
    in_sum = all_sum[1:].reshape(2, shards, d_own // zs, ff_block).swapaxes(0, 1)
    in_piece = exchange(in_sum, place, grads_ext).swapaxes(0, 1)
    all_piece = jnp.concatenate(
        [all_sum[:1], in_piece.reshape(2, block_rows_out, ff_block)], axis=0
    )
    all_all = from_rep(all_piece)
    grad_query_lin = undo_rope(
        grad_queries.reshape(tok_rows, HEADS, HEAD_DIM), cosine, sine_table
    ).reshape(tok_rows, D)
    grad_key_lin = undo_rope(
        grad_kv[:, :kv_width].reshape(tok_rows, KV_HEADS, HEAD_DIM), cosine, sine_table
    ).reshape(tok_rows, kv_width)
    grad_qkv = jnp.concatenate([grad_query_lin, grad_key_lin, grad_kv[:, kv_width:]], axis=1)
    grad_b_qkv = jnp.sum(grad_qkv, axis=0)
    qkv_low = after(grad_qkv.astype(jnp.bfloat16), layer_out)
    grad_attn_normed = jnp.einsum(
        "te,de->td", qkv_low, full_qkv, preferred_element_type=jnp.float32
    )
    grad_front, grad_attn_gain = rms_backward(grad_attn_normed, normed_attn, inv_attn, gain_attn)
    grad_input = grad_after + grad_front

    vectors = jnp.concatenate([grad_attn_gain, grad_b_qkv, grad_mlp_gain])
    vectors = vectors + swap(vectors, core_steps[0])
    ends = [0, D, 2 * D, 2 * D + kv_width, qkv_width + D, qkv_width + 2 * D]
    vectors = jnp.concatenate(
        [vectors[a:b].reshape(shards, -1) for a, b in zip(ends[:-1], ends[1:])], axis=1
    )
    vectors = pick(vectors.reshape(shards, CORES, zs, 1, -1), core, 1).astype(jnp.bfloat16)
    vector_len = vectors.shape[-1]
    piece_rows = d_own // CORES // zs
    below = 16 - piece_rows % 16
    vectors = jnp.pad(vectors, ((0, 0), (0, 0), (0, below - 1), (0, qkv_width - vector_len)))
    query_parts = half_sum(attn_input, qkv_low).reshape(shards, zs, piece_rows, qkv_width)
    query_parts = jnp.concatenate([query_parts, vectors], axis=2)
    query_sum = shard_scatter(query_parts.reshape(-1, qkv_width))
    out_sum = out_sum.reshape(zs, piece_rows, D)
    out_sum = jnp.pad(out_sum, ((0, 0), (0, below), (0, 0))).reshape(-1, D)
    parts = jnp.concatenate([query_sum.reshape(-1, qkv_width), out_sum], axis=1)
    y_halves = (2,) * len(y_steps)
    parts = scatter(parts.reshape(parts.shape[:1] + y_halves + (-1,)), place, y_steps, 1)
    piece = scatter(parts.reshape(z_halves + (-1, parts.shape[1])), place, z_steps)
    for index, step in enumerate(y_steps[::-1]):
        mine = jnp.expand_dims(piece, index + 1)
        got = jnp.expand_dims(swap(piece, step), index + 1)
        piece = ordered(mine, got, place, step, index + 1)
    piece = piece.reshape(piece.shape[0], -1)
    if by_tiles:
        final_gate, final_up, final_down = weights_in_place(all_all, shards, ff_own)
    attn_half = piece
    for index, step in enumerate(z_steps[::-1]):
        mine = jnp.expand_dims(attn_half, index)
        got = jnp.expand_dims(swap(attn_half, step), index)
        if by_tiles and index == len(z_steps) - 1:
            got = after(got, final_down)
        attn_half = ordered(mine, got, place, step, index)
    attn_half = attn_half.reshape(-1, attn_half.shape[-1])
    attn_other = swap(attn_half, core_steps[0])
    attn_all = ordered(attn_half, attn_other, place, core_steps[0])
    attn_all = attn_all.reshape(CORES * zs, piece_rows + below, qkv_width + D)
    vector_own = attn_all[:, piece_rows, :vector_len].reshape(-1).astype(jnp.float32)
    attn_all = attn_all[:, :piece_rows].reshape(d_own, qkv_width + D)
    edges = [0, D, D + kv_width, qkv_width, qkv_width + D]
    final_query, final_key, final_value, final_out = [
        attn_all[:, a:b].astype(jnp.float32) for a, b in zip(edges[:-1], edges[1:])
    ]
    final_gain, final_bq, final_bk, final_bv, final_mlp_gain = [
        vector_own[a:b] for a, b in zip(cuts[:-1], cuts[1:])
    ]

    if not by_tiles:
        kept = [slice(kept_of(index, ff_block, ff_own)[1], ff_block) for index in range(blocks)]
        down_all = from_block(all_all[:, :, 0])
        in_all = all_all[:, :, 1:].reshape(zs, blocks, 2, shards, d_own // zs, ff_block)

        def in_place(pieces):
            columns = []
            for owner in range(shards):
                for index in range(blocks):
                    whole = pieces[:, index, owner].reshape(d_own, ff_block)
                    columns.append(whole[:, kept[index]])
            return jnp.concatenate(columns, axis=1).astype(jnp.float32)

        final_down = jnp.concatenate(
            [down_all[:, index].reshape(ff_block, D)[kept[index]] for index in range(blocks)], axis=0
        ).astype(jnp.float32)
        final_gate = in_place(in_all[:, :, 0])
        final_up = in_place(in_all[:, :, 1])
    return (
        layer_out,
        grad_input,
        final_gain,
        final_query,
        final_bq,
        final_key,
        final_bk,
        final_value,
        final_bv,
        final_out,
        final_mlp_gain,
        final_gate,
        final_up,
        final_down,
    )


def solution(mesh):
    return jax.shard_map(
        per_device,
        mesh=mesh,
        in_specs=(
            P(("rep", "shard"), None),
            P(("rep", "shard")),
            P("shard"),
            P("shard", None),
            P("shard"),
            P("shard", None),
            P("shard"),
            P("shard", None),
            P("shard"),
            P("shard", None),
            P("shard"),
            P("shard", None),
            P("shard", None),
            P("shard", None),
            P(("rep", "shard"), None),
        ),
        out_specs=(
            P(("rep", "shard"), None),
            P(("rep", "shard"), None),
            P("shard"),
            P("shard", None),
            P("shard"),
            P("shard", None),
            P("shard"),
            P("shard", None),
            P("shard"),
            P("shard", None),
            P("shard"),
            P("shard", None),
            P("shard", None),
            P("shard", None),
        ),
        check_vma=False,
    )
```

profile of v0, /device:TPU:0, one launch (start us, length us, event | category | flops | bytes accessed | tf_op | source)
XLA Modules:
  0.0 393.1 jit_solution(6376378917653593831)
XLA Ops:
  7.9 4.9 %collective-permute-start = (s32[128]{0:T(128)S(1)}, s32[128]{0:T(128)S(1)}, u32[]{:S(2)}, u32[]{:S(2)}) collective-permute-start(s32[128]{0:T(128)S(1)} %get-tuple-element.82), channel_id=1, source_target_pairs={{0,4},{1,5},{2,6},{3,7},{4,8},{5,9},{6,10},{7,11},{8,12},{9,13},{1... | collective-permute-start | bytes 1544 | tf_op jit(solution)/shard_map/ppermute | solution.py:28
  16.2 3.7 constant_dynamic-slice_fusion.2
  25.8 12.3 %collective-permute-done.1.refs_0_ = bf16[240,1152]{1,0:T(8,128)(2,1)S(1)} collective-permute-done((bf16[240,1152]{1,0:T(8,128)(2,1)S(1)}, bf16[240,1152]{1,0:T(8,128)(2,1)S(1)}, u32[]{:S(2)}, u32[]{:S(2)}) %collective-permute-start.1) | collective-permute-done | bytes 552992 | tf_op jit(solution)/shard_map/ppermute | solution.py:54
  51.9 3.9 collective-permute-start.3
  57.5 3.7 collective-permute-done.4.refs_1_
  62.8 4.0 %collective-permute-done.7.refs_1_ = bf16[224,640]{1,0:T(8,128)(2,1)} collective-permute-done((bf16[224,640]{1,0:T(8,128)(2,1)S(1)}, bf16[224,640]{1,0:T(8,128)(2,1)}, u32[]{:S(2)}, u32[]{:S(2)}) %collective-permute-start.7) | collective-permute-done | bytes 286752 | tf_op jit(solution)/shard_map/ppermute | solution.py:54
  73.2 3.5 collective-permute-done.5
  96.1 4.1 %collective-permute-done.14 = bf16[128,896]{1,0:T(8,128)(2,1)S(1)} collective-permute-done((bf16[128,896]{1,0:T(8,128)(2,1)}, bf16[128,896]{1,0:T(8,128)(2,1)S(1)}, u32[]{:S(2)}, u32[]{:S(2)}) %collective-permute-start.14) | collective-permute-done | bytes 229408 | tf_op jit(solution)/shard_map/ppermute | solution.py:54
  102.5 11.2 %collective-permute-done.16 = bf16[256,896]{1,0:T(8,128)(2,1)S(1)} collective-permute-done((bf16[256,896]{1,0:T(8,128)(2,1)}, bf16[256,896]{1,0:T(8,128)(2,1)S(1)}, u32[]{:S(2)}, u32[]{:S(2)}) %collective-permute-start.16) | collective-permute-done | bytes 458784 | tf_op jit(solution)/shard_map/ppermute | solution.py:61
  119.4 3.0 fusion.54
  122.5 3.0 fusion.52
  125.5 3.9 multiply_convert_fusion
  135.7 7.7 %weight_sums.1 = bf16[4,3,224,640]{3,2,1,0:T(8,128)(2,1)} custom-call(bf16[1024,896]{1,0:T(8,128)(2,1)S(1)} %pad_maximum_fusion.x_ref, bf16[1024,896]{1,0:T(8,128)(2,1)} %pad_maximum_fusion.1.cot_ref, bf16[1024,640]{1,0:T(8,128)(2,1)S(1)} %get-tuple-element.28.refs_0_.hidden_ref, bf16[1024,640]{1,0:T(8,128)(2,1)S(1)} %get-tuple-element.27.gate_ref, ...), custom_call_target="tpu_custom_call" | custom-call | flops 3523215360 | bytes 12582912 | tf_op jit(solution)/shard_map/weight_sums/pallas_call | solution.py:237
  146.7 11.9 %collective-permute-done.20 = bf16[256,896]{1,0:T(8,128)(2,1)S(1)} collective-permute-done((bf16[256,896]{1,0:T(8,128)(2,1)S(1)}, bf16[256,896]{1,0:T(8,128)(2,1)S(1)}, u32[]{:S(2)}, u32[]{:S(2)}) %collective-permute-start.20) | collective-permute-done | bytes 458784 | tf_op jit(solution)/shard_map/ppermute | solution.py:61
  161.0 4.7 %collective-permute-done.21 = bf16[128,896]{1,0:T(8,128)(2,1)S(1)} collective-permute-done((bf16[128,896]{1,0:T(8,128)(2,1)S(1)}, bf16[128,896]{1,0:T(8,128)(2,1)S(1)}, u32[]{:S(2)}, u32[]{:S(2)}) %collective-permute-start.21) | collective-permute-done | bytes 229408 | tf_op jit(solution)/shard_map/ppermute | solution.py:54
  167.5 3.5 fusion.42
  176.7 3.6 fusion.8
  180.3 4.0 %fusion.2 = bf16[2,7,128,640]{2,3,1,0:T(8,128)(2,1)S(1)} fusion(f32[2,640,128,7]{2,1,3,0:T(8,128)} %copy-done.4, f32[2,7,128]{2,1,0:T(8,128)S(1)} %bitcast.251, f32[2,7,128]{2,1,0:T(8,128)S(1)} %log_add_fusion, pred[128,640]{0,1:T(8,128)(4,1)S(1)} %compare_and_fusion, bf16[640,2,64,1]{0,2,3,1:T(8,128)(2,1)S(1)} %bitcast.244, ...), kind=kOutput, calls=%fused_computation.3 | convolution fusion | flops 154828800 | bytes 7370752 | tf_op jit(solution)/shard_map/qkgd,wkd->kgqw/dot_general | solution.py:609
  196.0 4.5 %collective-permute-done.27 = bf16[224,896]{1,0:T(8,128)(2,1)S(1)} collective-permute-done((bf16[224,896]{1,0:T(8,128)(2,1)S(1)}, bf16[224,896]{1,0:T(8,128)(2,1)S(1)}, u32[]{:S(2)}, u32[]{:S(2)}) %collective-permute-start.27) | collective-permute-done | bytes 401440 | tf_op jit(solution)/shard_map/ppermute | solution.py:54
  201.4 6.3 %reduce-scatter.2.cloned.1.call-done = bf16[1,3,224,640]{3,2,1,0:T(8,128)(2,1)} async-done(((bf16[4,3,224,640]{3,2,1,0:T(8,128)(2,1)}), bf16[1,3,224,640]{3,2,1,0:T(8,128)(2,1)}) %reduce-scatter.2.cloned.1.call-update) | async-done | bytes 860176 | tf_op jit(solution)/shard_map/reduce_scatter | solution.py:569
  214.2 4.3 %collective-permute-done.42.refs_0_ = bf16[2,112,640]{2,1,0:T(8,128)(2,1)} collective-permute-done((bf16[2,112,640]{2,1,0:T(8,128)(2,1)}, bf16[2,112,640]{2,1,0:T(8,128)(2,1)}, u32[]{:S(2)}, u32[]{:S(2)}) %collective-permute-start.42) | collective-permute-done | bytes 286752 | tf_op jit(solution)/shard_map/ppermute | solution.py:54
  235.6 3.5 collective-permute-done.29
  242.9 3.9 fusion.33
  250.6 3.2 collective-permute-start.35
  253.8 14.5 %collective-permute-done.35 = bf16[256,1152]{1,0:T(8,128)(2,1)S(1)} collective-permute-done((bf16[256,1152]{1,0:T(8,128)(2,1)S(1)}, bf16[256,1152]{1,0:T(8,128)(2,1)S(1)}, u32[]{:S(2)}, u32[]{:S(2)}) %collective-permute-start.35) | collective-permute-done | bytes 589856 | tf_op jit(solution)/shard_map/ppermute | solution.py:54
  269.2 18.6 %collective-permute-start.36 = (bf16[256,1024]{0,1:T(8,128)(2,1)S(1)}, bf16[256,1024]{0,1:T(8,128)(2,1)S(1)}, u32[]{:S(2)}, u32[]{:S(2)}) collective-permute-start(bf16[256,1024]{0,1:T(8,128)(2,1)S(1)} %dynamic-slice_bitcast_fusion.1), channel_id=1, source_target_pairs={{0,4},{2,6},{4,0},{6,2},{8,12},{10,14},{12,8},{14,10},{16,20},{18,... | collective-permute-start | bytes 1572872 | tf_op jit(solution)/shard_map/ppermute | solution.py:61
  287.8 23.7 %collective-permute-done.36 = bf16[256,1024]{0,1:T(8,128)(2,1)S(1)} collective-permute-done((bf16[256,1024]{0,1:T(8,128)(2,1)S(1)}, bf16[256,1024]{0,1:T(8,128)(2,1)S(1)}, u32[]{:S(2)}, u32[]{:S(2)}) %collective-permute-start.36) | collective-permute-done | bytes 524320 | tf_op jit(solution)/shard_map/ppermute | solution.py:61
  312.6 11.4 %collective-permute-done.37 = bf16[2,64,1024]{2,1,0:T(8,128)(2,1)S(1)} collective-permute-done((bf16[2,64,1024]{2,1,0:T(8,128)(2,1)S(1)}, bf16[2,64,1024]{2,1,0:T(8,128)(2,1)S(1)}, u32[]{:S(2)}, u32[]{:S(2)}) %collective-permute-start.37) | collective-permute-done | bytes 262176 | tf_op jit(solution)/shard_map/ppermute | solution.py:61
  324.2 16.9 %collective-permute-done.38 = bf16[64,1024]{1,0:T(8,128)(2,1)S(1)} collective-permute-done((bf16[64,1024]{1,0:T(8,128)(2,1)S(1)}, bf16[64,1024]{1,0:T(8,128)(2,1)S(1)}, u32[]{:S(2)}, u32[]{:S(2)}) %collective-permute-start.38) | collective-permute-done | bytes 131104 | tf_op jit(solution)/shard_map/ppermute | solution.py:61
  343.9 2.9 collective-permute-done.39
  347.5 12.9 %collective-permute-done.40 = bf16[64,2048]{1,0:T(8,128)(2,1)S(1)} collective-permute-done((bf16[64,2048]{1,0:T(8,128)(2,1)S(1)}, bf16[64,2048]{1,0:T(8,128)(2,1)S(1)}, u32[]{:S(2)}, u32[]{:S(2)}) %collective-permute-start.40) | collective-permute-done | bytes 262176 | tf_op jit(solution)/shard_map/ppermute | solution.py:61
  360.9 15.0 %weights_in_place.1 = (f32[448,4864]{1,0:T(8,128)}, f32[448,4864]{1,0:T(8,128)}, f32[2432,896]{1,0:T(8,128)}) custom-call(bf16[4,4,3,224,640]{4,3,2,1,0:T(8,128)(2,1)} %bitcast.190), custom_call_target="tpu_custom_call" | custom-call | bytes 46137344 | tf_op jit(solution)/shard_map/weights_in_place/pallas_call | solution.py:297
  (437 shorter events, 138.9 us)
Async XLA Ops:
  7.2 200.5 %reduce-scatter.2.cloned.1.call-start = ((), (), s32[]{:S(2)}) async-start(), calls=%async_computation.1 | async-start | bytes 4300800 | tf_op jit(solution)/shard_map/reduce_scatter | solution.py:569
  7.9 15.9 %collective-permute-start = (s32[128]{0:T(128)S(1)}, s32[128]{0:T(128)S(1)}, u32[]{:S(2)}, u32[]{:S(2)}) collective-permute-start(s32[128]{0:T(128)S(1)} %get-tuple-element.82), channel_id=1, source_target_pairs={{0,4},{1,5},{2,6},{3,7},{4,8},{5,9},{6,10},{7,11},{8,12},{9,13},{1... | collective-permute-start | bytes 1544 | tf_op jit(solution)/shard_map/ppermute | solution.py:28
  24.1 14.1 %collective-permute-start.1 = (bf16[240,1152]{1,0:T(8,128)(2,1)S(1)}, bf16[240,1152]{1,0:T(8,128)(2,1)S(1)}, u32[]{:S(2)}, u32[]{:S(2)}) collective-permute-start(bf16[240,1152]{1,0:T(8,128)(2,1)S(1)} %pad_maximum_fusion.8), channel_id=1, source_target_pairs={{0,1},{1,0},{2,3},{3,2},{4,5},{5,4},{6,7},{7,6},{8,9},{9,8},{10,11... | collective-permute-start | bytes 1658888 | tf_op jit(solution)/shard_map/ppermute | solution.py:54
  42.0 27.3 %collective-permute-start.9 = (bf16[112,896]{1,0:T(8,128)(2,1)}, bf16[112,896]{1,0:T(8,128)(2,1)}, u32[]{:S(2)}, u32[]{:S(2)}) collective-permute-start(bf16[112,896]{1,0:T(8,128)(2,1)} %after.21), channel_id=1, source_target_pairs={{0,1},{1,0},{2,3},{3,2},{4,5},{5,4},{6,7},{7,6},{8,9},{9,8},{10,11... | collective-permute-start | bytes 602120 | tf_op jit(solution)/shard_map/ppermute | solution.py:54
  43.5 12.3 %collective-permute-start.8 = (bf16[128,896]{1,0:T(8,128)(2,1)}, bf16[128,896]{1,0:T(8,128)(2,1)S(1)}, u32[]{:S(2)}, u32[]{:S(2)}) collective-permute-start(bf16[128,896]{1,0:T(8,128)(2,1)} %after.19), channel_id=1, source_target_pairs={{0,1},{1,0},{2,3},{3,2},{4,5},{5,4},{6,7},{7,6},{8,9},{9,8},{10,11... | collective-permute-start | bytes 688136 | tf_op jit(solution)/shard_map/ppermute | solution.py:54
  44.0 17.2 %collective-permute-start.4 = (bf16[224,640]{1,0:T(8,128)(2,1)}, bf16[224,640]{1,0:T(8,128)(2,1)}, u32[]{:S(2)}, u32[]{:S(2)}) collective-permute-start(bf16[224,640]{1,0:T(8,128)(2,1)} %after.16), channel_id=1, source_target_pairs={{0,1},{1,0},{2,3},{3,2},{4,5},{5,4},{6,7},{7,6},{8,9},{9,8},{10,11... | collective-permute-start | bytes 860168 | tf_op jit(solution)/shard_map/ppermute | solution.py:54
  45.5 21.2 %collective-permute-start.7 = (bf16[224,640]{1,0:T(8,128)(2,1)S(1)}, bf16[224,640]{1,0:T(8,128)(2,1)}, u32[]{:S(2)}, u32[]{:S(2)}) collective-permute-start(bf16[224,640]{1,0:T(8,128)(2,1)S(1)} %copy-done.15), channel_id=1, source_target_pairs={{0,1},{1,0},{2,3},{3,2},{4,5},{5,4},{6,7},{7,6},{8,9},{9,8},{10,11... | collective-permute-start | bytes 860168 | tf_op jit(solution)/shard_map/ppermute | solution.py:54
  51.9 19.0 %collective-permute-start.3 = (bf16[128,256]{1,0:T(8,128)(2,1)S(1)}, bf16[128,256]{1,0:T(8,128)(2,1)S(1)}, u32[]{:S(2)}, u32[]{:S(2)}) collective-permute-start(bf16[128,256]{1,0:T(8,128)(2,1)S(1)} %get-tuple-element.57.refs_1_), channel_id=1, source_target_pairs={{0,4},{1,5},{2,6},{3,7},{4,8},{5,9},{6,10},{7,11},{8,12},{9,13},{1... | collective-permute-start | bytes 196616 | tf_op jit(solution)/shard_map/ppermute | solution.py:28
  55.9 24.0 %collective-permute-start.13 = (bf16[256,896]{1,0:T(8,128)(2,1)S(1)}, bf16[256,896]{1,0:T(8,128)(2,1)S(1)}, u32[]{:S(2)}, u32[]{:S(2)}) collective-permute-start(bf16[256,896]{1,0:T(8,128)(2,1)S(1)} %pad_maximum_fusion.10.refs_2_), channel_id=1, source_target_pairs={{0,4},{2,6},{4,0},{6,2},{8,12},{10,14},{12,8},{14,10},{16,20},{18,... | collective-permute-start | bytes 1376264 | tf_op jit(solution)/shard_map/ppermute | solution.py:61
  61.2 16.6 %collective-permute-start.12 = (bf16[224,640]{1,0:T(8,128)(2,1)}, bf16[224,640]{1,0:T(8,128)(2,1)S(1)}, u32[]{:S(2)}, u32[]{:S(2)}) collective-permute-start(bf16[224,640]{1,0:T(8,128)(2,1)} %collective-permute-done.4.refs_1_), channel_id=1, source_target_pairs={{0,8},{2,10},{4,12},{6,14},{8,0},{10,2},{12,4},{14,6},{16,24},{18,... | collective-permute-start | bytes 860168 | tf_op jit(solution)/shard_map/ppermute | solution.py:61
  66.8 27.1 %collective-permute-start.15 = (bf16[224,640]{1,0:T(8,128)(2,1)}, bf16[224,640]{1,0:T(8,128)(2,1)}, u32[]{:S(2)}, u32[]{:S(2)}) collective-permute-start(bf16[224,640]{1,0:T(8,128)(2,1)} %collective-permute-done.7.refs_1_), channel_id=1, source_target_pairs={{0,8},{2,10},{4,12},{6,14},{8,0},{10,2},{12,4},{14,6},{16,24},{18,... | collective-permute-start | bytes 860168 | tf_op jit(solution)/shard_map/ppermute | solution.py:61
  69.4 11.6 %collective-permute-start.10 = (bf16[112,896]{1,0:T(8,128)(2,1)}, bf16[112,896]{1,0:T(8,128)(2,1)S(1)}, u32[]{:S(2)}, u32[]{:S(2)}) collective-permute-start(bf16[112,896]{1,0:T(8,128)(2,1)} %after.22), channel_id=1, source_target_pairs={{0,4},{2,6},{4,0},{6,2},{8,12},{10,14},{12,8},{14,10},{16,20},{18,... | collective-permute-start | bytes 602120 | tf_op jit(solution)/shard_map/ppermute | solution.py:61
  101.9 11.8 %collective-permute-start.16 = (bf16[256,896]{1,0:T(8,128)(2,1)}, bf16[256,896]{1,0:T(8,128)(2,1)S(1)}, u32[]{:S(2)}, u32[]{:S(2)}) collective-permute-start(bf16[256,896]{1,0:T(8,128)(2,1)} %after.24), channel_id=1, source_target_pairs={{0,4},{2,6},{4,0},{6,2},{8,12},{10,14},{12,8},{14,10},{16,20},{18,... | collective-permute-start | bytes 1376264 | tf_op jit(solution)/shard_map/ppermute | solution.py:61
  102.5 14.1 %collective-permute-start.18 = (bf16[512,896]{1,0:T(8,128)(2,1)S(1)}, bf16[512,896]{1,0:T(8,128)(2,1)}, u32[]{:S(2)}, u32[]{:S(2)}) collective-permute-start(bf16[512,896]{1,0:T(8,128)(2,1)S(1)} %copy-done.12), channel_id=1, source_target_pairs={{0,2},{2,0},{4,6},{6,4},{8,10},{10,8},{12,14},{14,12},{16,18},{18,... | collective-permute-start | bytes 2752520 | tf_op jit(solution)/shard_map/ppermute | solution.py:61
  133.2 10.5 %collective-permute-start.19 = (f32[512,896]{1,0:T(8,128)S(1)}, f32[512,896]{1,0:T(8,128)}, u32[]{:S(2)}, u32[]{:S(2)}) collective-permute-start(f32[512,896]{1,0:T(8,128)S(1)} %slice.301), channel_id=1, source_target_pairs={{0,2},{2,0},{4,6},{6,4},{8,10},{10,8},{12,14},{14,12},{16,18},{18,... | collective-permute-start | bytes 5505032 | tf_op jit(solution)/shard_map/ppermute | solution.py:61
  143.4 217.5 %all-gather.3.cloned.1.call-start = ((), (), s32[]{:S(2)}) async-start(), calls=%async_computation.2 | async-start | bytes 14622720 | tf_op jit(solution)/shard_map/all_gather | solution.py:575
  146.0 12.6 %collective-permute-start.20 = (bf16[256,896]{1,0:T(8,128)(2,1)S(1)}, bf16[256,896]{1,0:T(8,128)(2,1)S(1)}, u32[]{:S(2)}, u32[]{:S(2)}) collective-permute-start(bf16[256,896]{1,0:T(8,128)(2,1)S(1)} %slice.384), channel_id=1, source_target_pairs={{0,4},{2,6},{4,0},{6,2},{8,12},{10,14},{12,8},{14,10},{16,20},{18,... | collective-permute-start | bytes 1376264 | tf_op jit(solution)/shard_map/ppermute | solution.py:61
  161.0 26.2 %collective-permute-start.25 = (bf16[128,2,224]{0,2,1:T(8,128)(2,1)}, bf16[128,2,224]{0,2,1:T(8,128)(2,1)}, u32[]{:S(2)}, u32[]{:S(2)}) collective-permute-start(bf16[128,2,224]{0,2,1:T(8,128)(2,1)} %get-tuple-element.52), channel_id=1, source_target_pairs={{0,2},{2,0},{4,6},{6,4},{8,10},{10,8},{12,14},{14,12},{16,18},{18,... | collective-permute-start | bytes 344072 | tf_op jit(solution)/shard_map/ppermute | solution.py:61
  167.5 19.7 %collective-permute-start.26 = (bf16[128,896]{1,0:T(8,128)(2,1)}, bf16[128,896]{1,0:T(8,128)(2,1)}, u32[]{:S(2)}, u32[]{:S(2)}) collective-permute-start(bf16[128,896]{1,0:T(8,128)(2,1)} %get-tuple-element.24.refs_1_), channel_id=1, source_target_pairs={{0,2},{2,0},{4,6},{6,4},{8,10},{10,8},{12,14},{14,12},{16,18},{18,... | collective-permute-start | bytes 688136 | tf_op jit(solution)/shard_map/ppermute | solution.py:61
  174.2 16.1 %collective-permute-start.22 = (f32[512,896]{1,0:T(8,128)}, f32[512,896]{1,0:T(8,128)}, u32[]{:S(2)}, u32[]{:S(2)}) collective-permute-start(f32[512,896]{1,0:T(8,128)} %slice.307), channel_id=1, source_target_pairs={{0,2},{2,0},{4,6},{6,4},{8,10},{10,8},{12,14},{14,12},{16,18},{18,... | collective-permute-start | bytes 5505032 | tf_op jit(solution)/shard_map/ppermute | solution.py:61
  188.8 11.8 %collective-permute-start.27 = (bf16[224,896]{1,0:T(8,128)(2,1)S(1)}, bf16[224,896]{1,0:T(8,128)(2,1)S(1)}, u32[]{:S(2)}, u32[]{:S(2)}) collective-permute-start(bf16[224,896]{1,0:T(8,128)(2,1)S(1)} %dynamic-slice_bitcast_fusion.3), channel_id=1, source_target_pairs={{0,1},{1,0},{2,3},{3,2},{4,5},{5,4},{6,7},{7,6},{8,9},{9,8},{10,11... | collective-permute-start | bytes 1204232 | tf_op jit(solution)/shard_map/ppermute | solution.py:54
  194.6 16.6 %collective-permute-start.23 = (bf16[256,896]{1,0:T(8,128)(2,1)}, bf16[256,896]{1,0:T(8,128)(2,1)}, u32[]{:S(2)}, u32[]{:S(2)}) collective-permute-start(bf16[256,896]{1,0:T(8,128)(2,1)} %slice.383), channel_id=1, source_target_pairs={{0,4},{2,6},{4,0},{6,2},{8,12},{10,14},{12,8},{14,10},{16,20},{18,... | collective-permute-start | bytes 1376264 | tf_op jit(solution)/shard_map/ppermute | solution.py:61
  209.7 8.7 %collective-permute-start.42 = (bf16[2,112,640]{2,1,0:T(8,128)(2,1)}, bf16[2,112,640]{2,1,0:T(8,128)(2,1)}, u32[]{:S(2)}, u32[]{:S(2)}) collective-permute-start(bf16[2,112,640]{2,1,0:T(8,128)(2,1)} %get-tuple-element.42), channel_id=1, source_target_pairs={{0,1},{1,0},{2,3},{3,2},{4,5},{5,4},{6,7},{7,6},{8,9},{9,8},{10,11... | collective-permute-start | bytes 860168 | tf_op jit(solution)/shard_map/ppermute | solution.py:54
  226.3 9.3 %collective-permute-start.28 = (f32[128,256]{1,0:T(8,128)S(1)}, f32[128,256]{1,0:T(8,128)S(1)}, u32[]{:S(2)}, u32[]{:S(2)}) collective-permute-start(f32[128,256]{1,0:T(8,128)S(1)} %get-tuple-element.37), channel_id=1, source_target_pairs={{4,0},{5,1},{6,2},{7,3},{8,4},{9,5},{10,6},{11,7},{12,8},{13,9},{1... | collective-permute-start | bytes 393224 | tf_op jit(solution)/shard_map/ppermute | solution.py:28
  230.2 9.0 %collective-permute-start.29 = (f32[128,256]{1,0:T(8,128)S(1)}, f32[128,256]{1,0:T(8,128)S(1)}, u32[]{:S(2)}, u32[]{:S(2)}) collective-permute-start(f32[128,256]{1,0:T(8,128)S(1)} %get-tuple-element.40), channel_id=1, source_target_pairs={{3,0},{4,1},{5,2},{6,3},{7,4},{8,5},{9,6},{10,7},{11,8},{12,9},{13... | collective-permute-start | bytes 393224 | tf_op jit(solution)/shard_map/ppermute | solution.py:28
  232.9 9.1 %collective-permute-start.24 = (bf16[128,896]{1,0:T(8,128)(2,1)S(1)}, bf16[128,896]{1,0:T(8,128)(2,1)S(1)}, u32[]{:S(2)}, u32[]{:S(2)}) collective-permute-start(bf16[128,896]{1,0:T(8,128)(2,1)S(1)} %slice.385), channel_id=1, source_target_pairs={{0,1},{1,0},{2,3},{3,2},{4,5},{5,4},{6,7},{7,6},{8,9},{9,8},{10,11... | collective-permute-start | bytes 688136 | tf_op jit(solution)/shard_map/ppermute | solution.py:54
  250.6 17.7 %collective-permute-start.35 = (bf16[256,1152]{1,0:T(8,128)(2,1)S(1)}, bf16[256,1152]{1,0:T(8,128)(2,1)S(1)}, u32[]{:S(2)}, u32[]{:S(2)}) collective-permute-start(bf16[256,1152]{1,0:T(8,128)(2,1)S(1)} %dynamic-slice_bitcast_fusion), channel_id=1, source_target_pairs={{0,1},{1,0},{2,3},{3,2},{4,5},{5,4},{6,7},{7,6},{8,9},{9,8},{10,11... | collective-permute-start | bytes 1769480 | tf_op jit(solution)/shard_map/ppermute | solution.py:54
  269.2 42.3 %collective-permute-start.36 = (bf16[256,1024]{0,1:T(8,128)(2,1)S(1)}, bf16[256,1024]{0,1:T(8,128)(2,1)S(1)}, u32[]{:S(2)}, u32[]{:S(2)}) collective-permute-start(bf16[256,1024]{0,1:T(8,128)(2,1)S(1)} %dynamic-slice_bitcast_fusion.1), channel_id=1, source_target_pairs={{0,4},{2,6},{4,0},{6,2},{8,12},{10,14},{12,8},{14,10},{16,20},{18,... | collective-permute-start | bytes 1572872 | tf_op jit(solution)/shard_map/ppermute | solution.py:61
  311.8 12.2 %collective-permute-start.37 = (bf16[2,64,1024]{2,1,0:T(8,128)(2,1)S(1)}, bf16[2,64,1024]{2,1,0:T(8,128)(2,1)S(1)}, u32[]{:S(2)}, u32[]{:S(2)}) collective-permute-start(bf16[2,64,1024]{2,1,0:T(8,128)(2,1)S(1)} %dynamic-slice_bitcast_fusion.8), channel_id=1, source_target_pairs={{0,8},{2,10},{4,12},{6,14},{8,0},{10,2},{12,4},{14,6},{16,24},{18,... | collective-permute-start | bytes 786440 | tf_op jit(solution)/shard_map/ppermute | solution.py:61
  324.1 16.9 %collective-permute-start.38 = (bf16[64,1024]{1,0:T(8,128)(2,1)S(1)}, bf16[64,1024]{1,0:T(8,128)(2,1)S(1)}, u32[]{:S(2)}, u32[]{:S(2)}) collective-permute-start(bf16[64,1024]{1,0:T(8,128)(2,1)S(1)} %dynamic-slice_bitcast_fusion.10), channel_id=1, source_target_pairs={{0,16},{2,18},{4,20},{6,22},{8,24},{10,26},{12,28},{14,30},{16,0},... | collective-permute-start | bytes 393224 | tf_op jit(solution)/shard_map/ppermute | solution.py:61
  346.9 13.5 %collective-permute-start.40 = (bf16[64,2048]{1,0:T(8,128)(2,1)S(1)}, bf16[64,2048]{1,0:T(8,128)(2,1)S(1)}, u32[]{:S(2)}, u32[]{:S(2)}) collective-permute-start(bf16[64,2048]{1,0:T(8,128)(2,1)S(1)} %bitcast.239), channel_id=1, source_target_pairs={{0,16},{2,18},{4,20},{6,22},{8,24},{10,26},{12,28},{14,30},{16,0},... | collective-permute-start | bytes 786440 | tf_op jit(solution)/shard_map/ppermute | solution.py:61
  360.5 15.3 %collective-permute-start.41 = (bf16[2,64,2048]{2,1,0:T(8,128)(2,1)S(1)}, bf16[2,64,2048]{2,1,0:T(8,128)(2,1)S(1)}, u32[]{:S(2)}, u32[]{:S(2)}) collective-permute-start(bf16[2,64,2048]{2,1,0:T(8,128)(2,1)S(1)} %maximum_select_fusion.13), channel_id=1, source_target_pairs={{0,8},{2,10},{4,12},{6,14},{8,0},{10,2},{12,4},{14,6},{16,24},{18,... | collective-permute-start | bytes 1572872 | tf_op jit(solution)/shard_map/ppermute | solution.py:61
  (91 other events, 548.3 us)
Sparse Core Ops, SparseCore 0:
  143.5 64.1 reduce-scatter.1
  220.9 138.8 all-gather.2
where the time goes:
time: 399 us; the launch traced here: 393 us
  waiting for transfers between devices  160 us (40%)
  starting transfers between devices  67.8 us (17%)
  other arithmetic  44.4 us (11%)
  local copies, waits for them, and re-layouts  42.5 us (11%)
  matrix products  39.3 us (10%)
  Pallas kernels  22.6 us (6%)
  between operations  16.2 us (4%)
    ppermute x26, waiting for transfers between devices, swap(): return lax.ppermute(value, 'rep', pairs)  93.1 us
    ppermute x12, waiting for transfers between devices, swap(): return lax.ppermute(value, 'shard', [(i, i ^ bit) for i in range(peers)])  57.1 us
    ppermute x26, starting transfers between devices, swap(): return lax.ppermute(value, 'rep', pairs)  34.4 us
    ppermute x12, starting transfers between devices, swap(): return lax.ppermute(value, 'shard', [(i, i ^ bit) for i in range(peers)])  19 us
    pallas_call x1, Pallas kernels, weights_in_place(): pl.pallas_call(kernel, grid=(zs,), out_shape=(wide, wide, jax.ShapeDtypeS...  15 us
    ppermute x6, starting transfers between devices, passed_along(): return lax.ppermute(shard, axis, pairs)  14.2 us
    unnamed x160, local copies, waits for them, and re-layouts  12 us
    select_n x16, other arithmetic, ordered(): jnp.where(first, jnp.concatenate([mine, got], axis=axis), jnp.concatenate...  10.9 us
  transfers between devices with their start and end apart: 46, of which 22 were waited for; matrix products, arithmetic and copies ran while one was open for 23% of the time, Pallas kernels for 6%

commit v1 on v0

--- a/solution.py
+++ b/solution.py
@@ -378,7 +378,13 @@
     block_at = jnp.minimum(block * ff_block, ff_own - ff_block)
 
     w_qkv = jnp.concatenate([w_query, w_key, w_value], axis=1)
-    qkv_half = pick(w_qkv.reshape(CORES, d_own // CORES, qkv_width), core)
+    qkv_half = jnp.concatenate(
+        [
+            pick(weight.reshape(CORES, d_own // CORES, -1), core)
+            for weight in (w_query, w_key, w_value)
+        ],
+        axis=1,
+    )
     small = jnp.concatenate([attn_gain, b_query, b_key, b_value, mlp_gain])
     own_segments = segments + 1
     group_is_reach = shards == 2 and CORES * shards == back_reach
@@ -402,18 +408,14 @@
         for weight in (w_gate, w_up)
     ]
     if group_is_reach:
+        got_qkv = swap(qkv_half, shard_steps[0])
         far = passed_along(own_segments, ("rep", "shard"), back_reach)
         both = jnp.concatenate([far, own_segments]).astype(jnp.bfloat16)
-        extra = -(-(small.shape[0] + 2 * tok_rows) // (16 * qkv_width)) * 16
-        sent = as_rows(jnp.concatenate([small, both]), extra)
-        got = swap(jnp.concatenate([qkv_half, sent], axis=0), shard_steps[0])
-        got = after(got, *columns_sent)
-        got_qkv, got_small = got[:-extra], got[-extra:].reshape(-1)
+        got_small = swap(jnp.concatenate([small, both]), shard_steps[0])
         small_all = ordered(small[None], got_small[None, : small.shape[0]], place, shard_steps[0])
-        got_both = got_small[small.shape[0] : small.shape[0] + 2 * tok_rows]
-        both = ordered(
-            both.reshape(2, 1, tok_rows), got_both.reshape(2, 1, tok_rows), place, shard_steps[0], 1
-        )
+        got_both = got_small[small.shape[0] :].reshape(2, 1, tok_rows)
+        both = ordered(both.reshape(2, 1, tok_rows), got_both, place, shard_steps[0], 1)
+        got_qkv = after(got_qkv, both, *columns_sent)
         sent = as_rows(both.reshape(-1), 16)
         other_qkv = swap(jnp.concatenate([got_qkv, sent], axis=0), core_steps[0])
         got_both = other_qkv[-16:].reshape(-1)[: both.size].reshape(2, 1, shards, tok_rows)
@@ -456,24 +458,19 @@
         return lax.all_gather(own, "shard", axis=0, tiled=True)
 
 
-    def block_rows(weight, sent, earlier):
-        own = columns_of(weight, shard)
+    def all_block_rows(weight, got):
         if shards == 2:
-            got = swap(after(sent, earlier), shard_steps[0])
             other = ordered(got, swap(got, z_steps[0]), place, z_steps[0])
-            return (ordered(own, other, place, shard_steps[0]), got, other)
+            return (ordered(columns_of(weight, shard), other, place, shard_steps[0]), other)
         sent = jnp.stack([columns_of(weight, owner) for owner in range(shards)])
         got = lax.all_to_all(sent, "shard", split_axis=0, concat_axis=0, tiled=True)
-        return (got.reshape(D, ff_block), got, got)
+        return (got.reshape(D, ff_block), got)
 
     out_part = pick(w_out.reshape(CORES, ys, d_own // CORES // ys, D), core)
     out_part = pick(out_part, place["y"])
     got_out = swap(after(out_part, got_qkv), shard_steps[0])
     cot_shards = group_tokens(after(cotangent, got_qkv), shard_steps)
-    cot_ys = group_tokens(cot_shards, y_steps)
-    cot_rows = group_tokens(cot_ys, core_steps)
-    gate_here, got_gate, other_gate = block_rows(w_gate, columns_sent[0], got_qkv)
-    up_here, got_up, other_up = block_rows(w_up, columns_sent[1], got_qkv)
+    got_gate, got_up = [swap(after(sent, got_qkv), shard_steps[0]) for sent in columns_sent]
     down_rows = lax.dynamic_slice_in_dim(w_down, block_at, ff_block, 0)
     once = block_at + jnp.arange(ff_block, dtype=jnp.int32) >= block * ff_block
     down_here = jnp.where(once[:, None], down_rows, jnp.zeros_like(down_rows))
@@ -487,14 +484,19 @@
     kv_own_rows = jnp.concatenate([rot[:, HEADS:].reshape(tok_rows, kv_width), value_low], axis=1)
     if group_is_reach:
         far = passed_along(kv_own_rows, ("rep", "shard"), back_reach)
-        both = after(jnp.stack([far, kv_own_rows])[:, None], got_gate)
+        both = jnp.stack([far, kv_own_rows])[:, None]
+        kv_sent = both
         both = ordered(both, swap(both, shard_steps[0]), place, shard_steps[0], 1)[:, None]
         both = ordered(both, swap(both, core_steps[0]), place, core_steps[0], 1)
         kv_ext = window(both)
     else:
         kv_ext = prior_rows(kv_own_rows, back_reach)
-    full_out = all_rows(w_out, after(got_out, kv_own_rows))
-    kv_ext = after(kv_ext, got_up, cot_shards)
+        kv_sent = kv_ext
+    full_out = all_rows(w_out, after(got_out, kv_sent))
+    gate_here, other_gate = all_block_rows(w_gate, after(got_gate, kv_sent))
+    up_here, other_up = all_block_rows(w_up, after(got_up, kv_sent))
+    cot_ys = group_tokens(after(cot_shards, kv_sent), y_steps)
+    cot_rows = group_tokens(cot_ys, core_steps)
     keys_ext = kv_ext[:, :kv_width].reshape(ext_len, KV_HEADS, HEAD_DIM)
     values_ext = kv_ext[:, kv_width:].reshape(ext_len, KV_HEADS, HEAD_DIM)
     queries = query_rot.reshape(tok_rows, KV_HEADS, head_group, HEAD_DIM)
@@ -510,13 +512,15 @@
     attn_rows = jnp.einsum(
         "kgqw,wkd->qkgd", probs_low, values_ext, preferred_element_type=jnp.float32
     ).astype(jnp.bfloat16)
-    attn_out = attn_rows.reshape(tok_rows, D)
+    attn_out = after(attn_rows.reshape(tok_rows, D), got_gate, got_up, cot_shards)
+    attn_rows = attn_out.reshape(attn_rows.shape)
     after_attn = input_wide + jnp.dot(attn_out, full_out, preferred_element_type=jnp.float32)
     normed_mlp, inv_mlp, scaled_mlp = rms_forward(after_attn, gain_mlp)
-    mlp_input = after(scaled_mlp.astype(jnp.bfloat16), other_gate, cot_ys)
+    mlp_input = scaled_mlp.astype(jnp.bfloat16)
 
     mlp_rows = group_tokens(mlp_input, shard_steps)
-    mlp_rows = group_tokens(after(mlp_rows, other_up), y_steps + core_steps)
+    mlp_rows = group_tokens(after(mlp_rows, other_gate, other_up, cot_ys), y_steps)
+    mlp_rows = group_tokens(after(mlp_rows, cot_rows), core_steps)
     gate_lin = jnp.dot(mlp_rows, gate_here, preferred_element_type=jnp.float32)
     up_lin = jnp.dot(mlp_rows, up_here, preferred_element_type=jnp.float32)
     gate_sig = jax.nn.sigmoid(gate_lin)

time: 399 us -> 388 us (0.972)
  waiting for transfers between devices: 160 us -> 138 us
  starting transfers between devices: 67.8 us -> 72.1 us
  other arithmetic: 44.4 us -> 48.6 us
    ppermute x12 -> x13, waiting for transfers between devices: 57.1 us -> 34.5 us  [swap(): return lax.ppermute(value, 'shard', [(i, i ^ bit) for i in range(peers)])]
    ppermute x26, waiting for transfers between devices: 93.1 us -> 102 us  [swap(): return lax.ppermute(value, 'rep', pairs)]
    reduce_scatter x1, waiting for transfers between devices: 6.34 us -> 0.01 us  [per_device(): lax.psum_scatter(all_parts, 'rep', scatter_dimension=0, axis_index_groups...]
    ppermute x12 -> x13, starting transfers between devices: 19 us -> 20.2 us  [swap(): return lax.ppermute(value, 'shard', [(i, i ^ bit) for i in range(peers)])]
    unnamed x160 -> x158, local copies, waits for them, and re-layouts: 12 us -> 10.9 us
  transfers between devices with their start and end apart: 46 -> 47, of which waited for: 22 -> 24; matrix products, arithmetic and copies ran while one was open for 23% -> 25% of each run, Pallas kernels for 6% -> 6%
where the time goes in v1:
time: 388 us; the launch traced here: 382 us
  waiting for transfers between devices  138 us (36%)
  starting transfers between devices  72.1 us (19%)
  other arithmetic  48.6 us (13%)
  local copies, waits for them, and re-layouts  43.3 us (11%)
  matrix products  41.5 us (11%)
  Pallas kernels  22.6 us (6%)
  between operations  16.2 us (4%)
    ppermute x26, waiting for transfers between devices, swap(): return lax.ppermute(value, 'rep', pairs)  102 us
    ppermute x26, starting transfers between devices, swap(): return lax.ppermute(value, 'rep', pairs)  37.2 us
    ppermute x13, waiting for transfers between devices, swap(): return lax.ppermute(value, 'shard', [(i, i ^ bit) for i in range(peers)])  34.5 us
    ppermute x13, starting transfers between devices, swap(): return lax.ppermute(value, 'shard', [(i, i ^ bit) for i in range(peers)])  20.2 us
    pallas_call x1, Pallas kernels, weights_in_place(): pl.pallas_call(kernel, grid=(zs,), out_shape=(wide, wide, jax.ShapeDtypeS...  15 us
    ppermute x6, starting transfers between devices, passed_along(): return lax.ppermute(shard, axis, pairs)  14.4 us
    unnamed x158, local copies, waits for them, and re-layouts  10.9 us
    concatenate x6, other arithmetic, group_tokens(): rows = jnp.concatenate([rows, swap(rows, step)], axis=0)  9.23 us
  transfers between devices with their start and end apart: 47, of which 24 were waited for; matrix products, arithmetic and copies ran while one was open for 25% of the time, Pallas kernels for 6%

profile of v1, /device:TPU:0, one launch (start us, length us, event | category | flops | bytes accessed | tf_op | source)
XLA Modules:
  0.0 382.3 jit_solution(16895791363509886394)
XLA Ops:
  8.1 4.9 %collective-permute-start = (s32[128]{0:T(128)S(1)}, s32[128]{0:T(128)S(1)}, u32[]{:S(2)}, u32[]{:S(2)}) collective-permute-start(s32[128]{0:T(128)S(1)} %get-tuple-element.84), channel_id=1, source_target_pairs={{0,4},{1,5},{2,6},{3,7},{4,8},{5,9},{6,10},{7,11},{8,12},{9,13},{1... | collective-permute-start | bytes 1544 | tf_op jit(solution)/shard_map/ppermute | solution.py:28
  17.7 4.3 %constant_dynamic-slice_fusion.2 = (bf16[448,640]{1,0:T(8,128)(2,1)}, bf16[448,640]{1,0:T(8,128)(2,1)S(1)}, bf16[448,640]{1,0:T(8,128)(2,1)S(1)}, bf16[448,640]{1,0:T(8,128)(2,1)}) fusion(bf16[448,4864]{1,0:T(8,128)(2,1)} %param.27, s32[]{:T(128)S(6)} %select_n.461, s32[]{:T(128)S(6)} %select_n.429, bf16[448,4864]{1,0:T(8,128)(2,1)} %param.26), kind=kLoop, calls=%fused_computation.182 | loop fusion | bytes 4587528 | tf_op jit(solution)/shard_map/dynamic_slice | solution.py:401
  24.9 4.3 %collective-permute-done.1 = bf16[1728]{0:T(1024)(128)(2,1)S(1)} collective-permute-done((bf16[1728]{0:T(1024)(128)(2,1)S(1)}, bf16[1728]{0:T(1024)(128)(2,1)S(1)}, u32[]{:S(2)}, u32[]{:S(2)}) %collective-permute-start.1) | collective-permute-done | bytes 3488 | tf_op jit(solution)/shard_map/ppermute | solution.py:54
  38.1 4.0 %collective-permute-start.4 = (bf16[128,256]{1,0:T(8,128)(2,1)S(1)}, bf16[128,256]{1,0:T(8,128)(2,1)S(1)}, u32[]{:S(2)}, u32[]{:S(2)}) collective-permute-start(bf16[128,256]{1,0:T(8,128)(2,1)S(1)} %get-tuple-element.59), channel_id=1, source_target_pairs={{0,4},{1,5},{2,6},{3,7},{4,8},{5,9},{6,10},{7,11},{8,12},{9,13},{1... | collective-permute-start | bytes 196616 | tf_op jit(solution)/shard_map/ppermute | solution.py:28
  54.8 3.5 collective-permute-done.11
  75.8 5.5 %collective-permute-done.16 = bf16[256,896]{1,0:T(8,128)(2,1)S(1)} collective-permute-done((bf16[256,896]{1,0:T(8,128)(2,1)}, bf16[256,896]{1,0:T(8,128)(2,1)S(1)}, u32[]{:S(2)}, u32[]{:S(2)}) %collective-permute-start.16) | collective-permute-done | bytes 458784 | tf_op jit(solution)/shard_map/ppermute | solution.py:61
  87.1 11.4 %collective-permute-done.17 = bf16[256,896]{1,0:T(8,128)(2,1)S(1)} collective-permute-done((bf16[256,896]{1,0:T(8,128)(2,1)}, bf16[256,896]{1,0:T(8,128)(2,1)S(1)}, u32[]{:S(2)}, u32[]{:S(2)}) %collective-permute-start.17) | collective-permute-done | bytes 458784 | tf_op jit(solution)/shard_map/ppermute | solution.py:61
  103.1 2.8 collective-permute-done.19
  105.9 3.4 fusion.54
  109.3 2.9 fusion.52
  112.3 4.1 %multiply_convert_fusion = (bf16[1024,640]{1,0:T(8,128)(2,1)S(1)}, bf16[1024,640]{1,0:T(8,128)(2,1)S(1)}, bf16[1024,640]{1,0:T(8,128)(2,1)S(1)}) fusion(f32[1024,640]{1,0:T(8,128)S(1)} %fusion.54, f32[1024,640]{1,0:T(8,128)S(1)} %fusion.52, bf16[2432,896]{1,0:T(8,128)(2,1)} %param.28, s32[]{:T(128)S(6)} %select_n.464, ...), kind=kOutput, calls=%fused_computation.11 | convolution fusion | flops 1190313984 | bytes 12157572 | tf_op jit(solution)/shard_map/td,fd->tf/dot_general | solution.py:530
  122.3 7.7 %weight_sums.1 = bf16[4,3,224,640]{3,2,1,0:T(8,128)(2,1)} custom-call(bf16[1024,896]{1,0:T(8,128)(2,1)S(1)} %pad_maximum_fusion.1.x_ref, bf16[1024,896]{1,0:T(8,128)(2,1)} %pad_maximum_fusion.refs_1_.cot_ref, bf16[1024,640]{1,0:T(8,128)(2,1)S(1)} %get-tuple-element.28.refs_0_.hidden_ref, bf16[1024,640]{1,0:T(8,128)(2,1)S(1)} %get-tuple-element.27.gate_ref, ...), custom_call_target="tpu_custom_call" | custom-call | flops 3523215360 | bytes 12582912 | tf_op jit(solution)/shard_map/weight_sums/pallas_call | solution.py:237
  135.0 11.4 %collective-permute-done.21 = bf16[256,896]{1,0:T(8,128)(2,1)} collective-permute-done((bf16[256,896]{1,0:T(8,128)(2,1)}, bf16[256,896]{1,0:T(8,128)(2,1)}, u32[]{:S(2)}, u32[]{:S(2)}) %collective-permute-start.21) | collective-permute-done | bytes 458784 | tf_op jit(solution)/shard_map/ppermute | solution.py:61
  151.7 3.9 %collective-permute-done.22 = bf16[128,896]{1,0:T(8,128)(2,1)S(1)} collective-permute-done((bf16[128,896]{1,0:T(8,128)(2,1)S(1)}, bf16[128,896]{1,0:T(8,128)(2,1)S(1)}, u32[]{:S(2)}, u32[]{:S(2)}) %collective-permute-start.22) | collective-permute-done | bytes 229408 | tf_op jit(solution)/shard_map/ppermute | solution.py:54
  159.2 3.5 fusion.42
  168.5 4.3 %fusion.8 = f32[2,64,640,1]{2,1,3,0:T(8,128)} fusion(bf16[128,2,7,64]{0,3,2,1:T(8,128)(2,1)S(1)} %bitcast.236, f32[2,640,128,7]{2,1,3,0:T(8,128)} %copy-done.4, f32[2,7,128]{2,1,0:T(8,128)S(1)} %log_add_fusion, pred[128,640]{0,1:T(8,128)(4,1)S(1)} %compare_and_fusion), kind=kOutput, calls=%fused_computation.20 | convolution fusion | flops 151388160 | bytes 5233664 | tf_op jit(solution)/shard_map/kgqw,qkgd->wkd/dot_general | solution.py:610
  172.8 4.0 %fusion.2 = bf16[2,7,128,640]{2,3,1,0:T(8,128)(2,1)S(1)} fusion(f32[2,640,128,7]{2,1,3,0:T(8,128)} %copy-done.4, f32[2,7,128]{2,1,0:T(8,128)S(1)} %bitcast.259, f32[2,7,128]{2,1,0:T(8,128)} %copy-done.65, pred[128,640]{0,1:T(8,128)(4,1)S(1)} %compare_and_fusion, bf16[640,2,64,1]{0,2,3,1:T(8,128)(2,1)S(1)} %bitcast.251, bf16[128,2,7,64]{0,3,2,1:T(8,128)(2,1)} %bitcast.237), kind=kOutput, calls=%fused_computation.3 | convolution fusion | flops 154828800 | bytes 7370752 | tf_op jit(solution)/shard_map/qkgd,wkd->kgqw/dot_general | solution.py:613
  191.2 3.5 collective-permute-done.28
  199.2 2.6 collective-permute-done.24
  223.8 2.6 collective-permute-start.25
  229.3 3.3 collective-permute-done.25
  233.5 3.9 %fusion.33 = (f32[896]{0:T(1024)S(1)}, f32[128]{0:T(128)S(1)}, f32[128,896]{1,0:T(8,128)}) fusion(bf16[128,896]{1,0:T(8,128)(2,1)S(1)} %copy-done.27, f32[128]{0:T(128)S(1)} %copy-done.73, f32[896]{0:T(1024)S(1)} %copy-done.61, bf16[128,1152]{1,0:T(8,128)(2,1)} %after.31, bf16[448,1152]{1,0:T(8,128)(2,1)} %copy-done.36, bf16[448,1152]{1,0:T(8,128)(2,1)} %copy-done.45, ...), kind=kOutput, calls=%fused_computation.90 | convolution fusion | flops 274332672 | bytes 3055617 | tf_op jit(solution)/shard_map/te,de->td/dot_general | solution.py:647
  241.5 3.8 collective-permute-start.36
  245.4 14.5 %collective-permute-done.36 = bf16[256,1152]{1,0:T(8,128)(2,1)} collective-permute-done((bf16[256,1152]{1,0:T(8,128)(2,1)S(1)}, bf16[256,1152]{1,0:T(8,128)(2,1)}, u32[]{:S(2)}, u32[]{:S(2)}) %collective-permute-start.36) | collective-permute-done | bytes 589856 | tf_op jit(solution)/shard_map/ppermute | solution.py:54
  261.9 20.2 %collective-permute-start.37 = (bf16[256,1024]{0,1:T(8,128)(2,1)S(1)}, bf16[256,1024]{0,1:T(8,128)(2,1)S(1)}, u32[]{:S(2)}, u32[]{:S(2)}) collective-permute-start(bf16[256,1024]{0,1:T(8,128)(2,1)S(1)} %dynamic-slice_bitcast_fusion.1), channel_id=1, source_target_pairs={{0,4},{2,6},{4,0},{6,2},{8,12},{10,14},{12,8},{14,10},{16,20},{18,... | collective-permute-start | bytes 1572872 | tf_op jit(solution)/shard_map/ppermute | solution.py:61
  282.2 23.7 %collective-permute-done.37 = bf16[256,1024]{0,1:T(8,128)(2,1)S(1)} collective-permute-done((bf16[256,1024]{0,1:T(8,128)(2,1)S(1)}, bf16[256,1024]{0,1:T(8,128)(2,1)S(1)}, u32[]{:S(2)}, u32[]{:S(2)}) %collective-permute-start.37) | collective-permute-done | bytes 524320 | tf_op jit(solution)/shard_map/ppermute | solution.py:61
  306.4 9.7 %collective-permute-done.38 = bf16[2,64,1024]{2,1,0:T(8,128)(2,1)S(1)} collective-permute-done((bf16[2,64,1024]{2,1,0:T(8,128)(2,1)S(1)}, bf16[2,64,1024]{2,1,0:T(8,128)(2,1)S(1)}, u32[]{:S(2)}, u32[]{:S(2)}) %collective-permute-start.38) | collective-permute-done | bytes 262176 | tf_op jit(solution)/shard_map/ppermute | solution.py:61
  316.2 15.4 %collective-permute-done.39 = bf16[64,1024]{1,0:T(8,128)(2,1)S(1)} collective-permute-done((bf16[64,1024]{1,0:T(8,128)(2,1)S(1)}, bf16[64,1024]{1,0:T(8,128)(2,1)S(1)}, u32[]{:S(2)}, u32[]{:S(2)}) %collective-permute-start.39) | collective-permute-done | bytes 131104 | tf_op jit(solution)/shard_map/ppermute | solution.py:61
  331.7 3.8 collective-permute-start.40
  335.4 2.9 collective-permute-done.40
  339.0 10.6 %collective-permute-done.41 = bf16[64,2048]{1,0:T(8,128)(2,1)S(1)} collective-permute-done((bf16[64,2048]{1,0:T(8,128)(2,1)S(1)}, bf16[64,2048]{1,0:T(8,128)(2,1)S(1)}, u32[]{:S(2)}, u32[]{:S(2)}) %collective-permute-start.41) | collective-permute-done | bytes 262176 | tf_op jit(solution)/shard_map/ppermute | solution.py:61
  350.1 15.0 %weights_in_place.1 = (f32[448,4864]{1,0:T(8,128)}, f32[448,4864]{1,0:T(8,128)}, f32[2432,896]{1,0:T(8,128)}) custom-call(bf16[4,4,3,224,640]{4,3,2,1,0:T(8,128)(2,1)} %bitcast.195), custom_call_target="tpu_custom_call" | custom-call | bytes 46137344 | tf_op jit(solution)/shard_map/weights_in_place/pallas_call | solution.py:297
  (437 shorter events, 144.8 us)
Async XLA Ops:
  7.2 188.4 %reduce-scatter.2.cloned.1.call-start = ((), (), s32[]{:S(2)}) async-start(), calls=%async_computation.1 | async-start | bytes 4300800 | tf_op jit(solution)/shard_map/reduce_scatter | solution.py:573
  8.1 16.2 %collective-permute-start = (s32[128]{0:T(128)S(1)}, s32[128]{0:T(128)S(1)}, u32[]{:S(2)}, u32[]{:S(2)}) collective-permute-start(s32[128]{0:T(128)S(1)} %get-tuple-element.84), channel_id=1, source_target_pairs={{0,4},{1,5},{2,6},{3,7},{4,8},{5,9},{6,10},{7,11},{8,12},{9,13},{1... | collective-permute-start | bytes 1544 | tf_op jit(solution)/shard_map/ppermute | solution.py:28
  15.7 13.8 %collective-permute-start.2 = (bf16[224,1152]{1,0:T(8,128)(2,1)}, bf16[224,1152]{1,0:T(8,128)(2,1)S(1)}, u32[]{:S(2)}, u32[]{:S(2)}) collective-permute-start(bf16[224,1152]{1,0:T(8,128)(2,1)} %pad_maximum_fusion.9), channel_id=1, source_target_pairs={{0,1},{1,0},{2,3},{3,2},{4,5},{5,4},{6,7},{7,6},{8,9},{9,8},{10,11... | collective-permute-start | bytes 1548296 | tf_op jit(solution)/shard_map/ppermute | solution.py:54
  33.2 14.7 %collective-permute-start.9 = (bf16[128,896]{1,0:T(8,128)(2,1)}, bf16[128,896]{1,0:T(8,128)(2,1)}, u32[]{:S(2)}, u32[]{:S(2)}) collective-permute-start(bf16[128,896]{1,0:T(8,128)(2,1)} %after.20), channel_id=1, source_target_pairs={{0,1},{1,0},{2,3},{3,2},{4,5},{5,4},{6,7},{7,6},{8,9},{9,8},{10,11... | collective-permute-start | bytes 688136 | tf_op jit(solution)/shard_map/ppermute | solution.py:54
  45.2 9.4 %collective-permute-start.5 = (bf16[2,1,128,256]{3,2,1,0:T(8,128)(2,1)S(1)}, bf16[2,1,128,256]{3,2,1,0:T(8,128)(2,1)S(1)}, u32[]{:S(2)}, u32[]{:S(2)}) collective-permute-start(bf16[2,1,128,256]{3,2,1,0:T(8,128)(2,1)S(1)} %get-tuple-element.56.refs_1_), channel_id=1, source_target_pairs={{0,1},{1,0},{2,3},{3,2},{4,5},{5,4},{6,7},{7,6},{8,9},{9,8},{10,11... | collective-permute-start | bytes 393224 | tf_op jit(solution)/shard_map/ppermute | solution.py:54
  45.9 19.4 %collective-permute-start.7 = (bf16[224,640]{1,0:T(8,128)(2,1)}, bf16[224,640]{1,0:T(8,128)(2,1)S(1)}, u32[]{:S(2)}, u32[]{:S(2)}) collective-permute-start(bf16[224,640]{1,0:T(8,128)(2,1)} %after.18), channel_id=1, source_target_pairs={{0,1},{1,0},{2,3},{3,2},{4,5},{5,4},{6,7},{7,6},{8,9},{9,8},{10,11... | collective-permute-start | bytes 860168 | tf_op jit(solution)/shard_map/ppermute | solution.py:54
  47.4 18.4 %collective-permute-start.8 = (bf16[224,640]{1,0:T(8,128)(2,1)}, bf16[224,640]{1,0:T(8,128)(2,1)S(1)}, u32[]{:S(2)}, u32[]{:S(2)}) collective-permute-start(bf16[224,640]{1,0:T(8,128)(2,1)} %after.19), channel_id=1, source_target_pairs={{0,1},{1,0},{2,3},{3,2},{4,5},{5,4},{6,7},{7,6},{8,9},{9,8},{10,11... | collective-permute-start | bytes 860168 | tf_op jit(solution)/shard_map/ppermute | solution.py:54
  59.5 10.8 %collective-permute-start.12 = (bf16[224,896]{1,0:T(8,128)(2,1)S(1)}, bf16[224,896]{1,0:T(8,128)(2,1)}, u32[]{:S(2)}, u32[]{:S(2)}) collective-permute-start(bf16[224,896]{1,0:T(8,128)(2,1)S(1)} %maximum_select_fusion.14), channel_id=1, source_target_pairs={{0,2},{2,0},{4,6},{6,4},{8,10},{10,8},{12,14},{14,12},{16,18},{18,... | collective-permute-start | bytes 1204232 | tf_op jit(solution)/shard_map/ppermute | solution.py:61
  66.7 14.8 %collective-permute-start.14 = (bf16[224,640]{1,0:T(8,128)(2,1)}, bf16[224,640]{1,0:T(8,128)(2,1)}, u32[]{:S(2)}, u32[]{:S(2)}) collective-permute-start(bf16[224,640]{1,0:T(8,128)(2,1)} %after.24), channel_id=1, source_target_pairs={{0,8},{2,10},{4,12},{6,14},{8,0},{10,2},{12,4},{14,6},{16,24},{18,... | collective-permute-start | bytes 860168 | tf_op jit(solution)/shard_map/ppermute | solution.py:61
  68.3 15.5 %collective-permute-start.15 = (bf16[224,640]{1,0:T(8,128)(2,1)}, bf16[224,640]{1,0:T(8,128)(2,1)S(1)}, u32[]{:S(2)}, u32[]{:S(2)}) collective-permute-start(bf16[224,640]{1,0:T(8,128)(2,1)} %after.25), channel_id=1, source_target_pairs={{0,8},{2,10},{4,12},{6,14},{8,0},{10,2},{12,4},{14,6},{16,24},{18,... | collective-permute-start | bytes 860168 | tf_op jit(solution)/shard_map/ppermute | solution.py:61
  68.7 12.6 %collective-permute-start.16 = (bf16[256,896]{1,0:T(8,128)(2,1)}, bf16[256,896]{1,0:T(8,128)(2,1)S(1)}, u32[]{:S(2)}, u32[]{:S(2)}) collective-permute-start(bf16[256,896]{1,0:T(8,128)(2,1)} %after.26), channel_id=1, source_target_pairs={{0,4},{2,6},{4,0},{6,2},{8,12},{10,14},{12,8},{14,10},{16,20},{18,... | collective-permute-start | bytes 1376264 | tf_op jit(solution)/shard_map/ppermute | solution.py:61
  74.2 10.5 %collective-permute-start.13 = (bf16[128,896]{1,0:T(8,128)(2,1)S(1)}, bf16[128,896]{1,0:T(8,128)(2,1)S(1)}, u32[]{:S(2)}, u32[]{:S(2)}) collective-permute-start(bf16[128,896]{1,0:T(8,128)(2,1)S(1)} %multiply_convert_fusion.3), channel_id=1, source_target_pairs={{0,1},{1,0},{2,3},{3,2},{4,5},{5,4},{6,7},{7,6},{8,9},{9,8},{10,11... | collective-permute-start | bytes 688136 | tf_op jit(solution)/shard_map/ppermute | solution.py:54
  81.4 19.1 %collective-permute-start.18 = (bf16[512,896]{1,0:T(8,128)(2,1)S(1)}, bf16[512,896]{1,0:T(8,128)(2,1)}, u32[]{:S(2)}, u32[]{:S(2)}) collective-permute-start(bf16[512,896]{1,0:T(8,128)(2,1)S(1)} %pad_maximum_fusion.3.refs_3_), channel_id=1, source_target_pairs={{0,2},{2,0},{4,6},{6,4},{8,10},{10,8},{12,14},{14,12},{16,18},{18,... | collective-permute-start | bytes 2752520 | tf_op jit(solution)/shard_map/ppermute | solution.py:61
  85.6 12.9 %collective-permute-start.17 = (bf16[256,896]{1,0:T(8,128)(2,1)}, bf16[256,896]{1,0:T(8,128)(2,1)S(1)}, u32[]{:S(2)}, u32[]{:S(2)}) collective-permute-start(bf16[256,896]{1,0:T(8,128)(2,1)} %after.27), channel_id=1, source_target_pairs={{0,4},{2,6},{4,0},{6,2},{8,12},{10,14},{12,8},{14,10},{16,20},{18,... | collective-permute-start | bytes 1376264 | tf_op jit(solution)/shard_map/ppermute | solution.py:61
  120.0 10.2 %collective-permute-start.20 = (f32[512,896]{1,0:T(8,128)S(1)}, f32[512,896]{1,0:T(8,128)}, u32[]{:S(2)}, u32[]{:S(2)}) collective-permute-start(f32[512,896]{1,0:T(8,128)S(1)} %slice.289), channel_id=1, source_target_pairs={{0,2},{2,0},{4,6},{6,4},{8,10},{10,8},{12,14},{14,12},{16,18},{18,... | collective-permute-start | bytes 5505032 | tf_op jit(solution)/shard_map/ppermute | solution.py:61
  130.0 220.1 %all-gather.3.cloned.1.call-start = ((), (), s32[]{:S(2)}) async-start(), calls=%async_computation.2 | async-start | bytes 14622720 | tf_op jit(solution)/shard_map/all_gather | solution.py:579
  133.3 13.1 %collective-permute-start.21 = (bf16[256,896]{1,0:T(8,128)(2,1)}, bf16[256,896]{1,0:T(8,128)(2,1)}, u32[]{:S(2)}, u32[]{:S(2)}) collective-permute-start(bf16[256,896]{1,0:T(8,128)(2,1)} %slice.372), channel_id=1, source_target_pairs={{0,4},{2,6},{4,0},{6,2},{8,12},{10,14},{12,8},{14,10},{16,20},{18,... | collective-permute-start | bytes 1376264 | tf_op jit(solution)/shard_map/ppermute | solution.py:61
  150.9 30.5 %collective-permute-start.26 = (bf16[128,2,224]{0,2,1:T(8,128)(2,1)}, bf16[128,2,224]{0,2,1:T(8,128)(2,1)}, u32[]{:S(2)}, u32[]{:S(2)}) collective-permute-start(bf16[128,2,224]{0,2,1:T(8,128)(2,1)} %get-tuple-element.52), channel_id=1, source_target_pairs={{0,2},{2,0},{4,6},{6,4},{8,10},{10,8},{12,14},{14,12},{16,18},{18,... | collective-permute-start | bytes 344072 | tf_op jit(solution)/shard_map/ppermute | solution.py:61
  159.2 22.2 %collective-permute-start.27 = (bf16[128,896]{1,0:T(8,128)(2,1)}, bf16[128,896]{1,0:T(8,128)(2,1)}, u32[]{:S(2)}, u32[]{:S(2)}) collective-permute-start(bf16[128,896]{1,0:T(8,128)(2,1)} %get-tuple-element.24.refs_1_), channel_id=1, source_target_pairs={{0,2},{2,0},{4,6},{6,4},{8,10},{10,8},{12,14},{14,12},{16,18},{18,... | collective-permute-start | bytes 688136 | tf_op jit(solution)/shard_map/ppermute | solution.py:61
  165.9 18.6 %collective-permute-start.23 = (f32[512,896]{1,0:T(8,128)}, f32[512,896]{1,0:T(8,128)}, u32[]{:S(2)}, u32[]{:S(2)}) collective-permute-start(f32[512,896]{1,0:T(8,128)} %slice.295), channel_id=1, source_target_pairs={{0,2},{2,0},{4,6},{6,4},{8,10},{10,8},{12,14},{14,12},{16,18},{18,... | collective-permute-start | bytes 5505032 | tf_op jit(solution)/shard_map/ppermute | solution.py:61
  183.0 11.8 %collective-permute-start.28 = (bf16[224,896]{1,0:T(8,128)(2,1)S(1)}, bf16[224,896]{1,0:T(8,128)(2,1)S(1)}, u32[]{:S(2)}, u32[]{:S(2)}) collective-permute-start(bf16[224,896]{1,0:T(8,128)(2,1)S(1)} %dynamic-slice_bitcast_fusion.2), channel_id=1, source_target_pairs={{0,1},{1,0},{2,3},{3,2},{4,5},{5,4},{6,7},{7,6},{8,9},{9,8},{10,11... | collective-permute-start | bytes 1204232 | tf_op jit(solution)/shard_map/ppermute | solution.py:54
  188.8 13.1 %collective-permute-start.24 = (bf16[256,896]{1,0:T(8,128)(2,1)}, bf16[256,896]{1,0:T(8,128)(2,1)}, u32[]{:S(2)}, u32[]{:S(2)}) collective-permute-start(bf16[256,896]{1,0:T(8,128)(2,1)} %slice.371), channel_id=1, source_target_pairs={{0,4},{2,6},{4,0},{6,2},{8,12},{10,14},{12,8},{14,10},{16,20},{18,... | collective-permute-start | bytes 1376264 | tf_op jit(solution)/shard_map/ppermute | solution.py:61
  197.8 8.9 %collective-permute-start.43 = (bf16[2,112,640]{2,1,0:T(8,128)(2,1)}, bf16[2,112,640]{2,1,0:T(8,128)(2,1)}, u32[]{:S(2)}, u32[]{:S(2)}) collective-permute-start(bf16[2,112,640]{2,1,0:T(8,128)(2,1)} %get-tuple-element.42), channel_id=1, source_target_pairs={{0,1},{1,0},{2,3},{3,2},{4,5},{5,4},{6,7},{7,6},{8,9},{9,8},{10,11... | collective-permute-start | bytes 860168 | tf_op jit(solution)/shard_map/ppermute | solution.py:54
  216.2 10.2 %collective-permute-start.29 = (f32[128,256]{1,0:T(8,128)S(1)}, f32[128,256]{1,0:T(8,128)S(1)}, u32[]{:S(2)}, u32[]{:S(2)}) collective-permute-start(f32[128,256]{1,0:T(8,128)S(1)} %get-tuple-element.37), channel_id=1, source_target_pairs={{4,0},{5,1},{6,2},{7,3},{8,4},{9,5},{10,6},{11,7},{12,8},{13,9},{1... | collective-permute-start | bytes 393224 | tf_op jit(solution)/shard_map/ppermute | solution.py:28
  217.6 8.8 %collective-permute-start.32 = (f32[128,256]{1,0:T(8,128)S(1)}, f32[128,256]{1,0:T(8,128)S(1)}, u32[]{:S(2)}, u32[]{:S(2)}) collective-permute-start(f32[128,256]{1,0:T(8,128)S(1)} %get-tuple-element.38), channel_id=1, source_target_pairs={{1,0},{2,1},{3,2},{4,3},{5,4},{6,5},{7,6},{8,7},{9,8},{10,9},{11,1... | collective-permute-start | bytes 393224 | tf_op jit(solution)/shard_map/ppermute | solution.py:28
  223.8 8.9 %collective-permute-start.25 = (bf16[128,896]{1,0:T(8,128)(2,1)}, bf16[128,896]{1,0:T(8,128)(2,1)S(1)}, u32[]{:S(2)}, u32[]{:S(2)}) collective-permute-start(bf16[128,896]{1,0:T(8,128)(2,1)} %slice.373), channel_id=1, source_target_pairs={{0,1},{1,0},{2,3},{3,2},{4,5},{5,4},{6,7},{7,6},{8,9},{9,8},{10,11... | collective-permute-start | bytes 688136 | tf_op jit(solution)/shard_map/ppermute | solution.py:54
  241.5 18.3 %collective-permute-start.36 = (bf16[256,1152]{1,0:T(8,128)(2,1)S(1)}, bf16[256,1152]{1,0:T(8,128)(2,1)}, u32[]{:S(2)}, u32[]{:S(2)}) collective-permute-start(bf16[256,1152]{1,0:T(8,128)(2,1)S(1)} %dynamic-slice_bitcast_fusion), channel_id=1, source_target_pairs={{0,1},{1,0},{2,3},{3,2},{4,5},{5,4},{6,7},{7,6},{8,9},{9,8},{10,11... | collective-permute-start | bytes 1769480 | tf_op jit(solution)/shard_map/ppermute | solution.py:54
  261.9 43.9 %collective-permute-start.37 = (bf16[256,1024]{0,1:T(8,128)(2,1)S(1)}, bf16[256,1024]{0,1:T(8,128)(2,1)S(1)}, u32[]{:S(2)}, u32[]{:S(2)}) collective-permute-start(bf16[256,1024]{0,1:T(8,128)(2,1)S(1)} %dynamic-slice_bitcast_fusion.1), channel_id=1, source_target_pairs={{0,4},{2,6},{4,0},{6,2},{8,12},{10,14},{12,8},{14,10},{16,20},{18,... | collective-permute-start | bytes 1572872 | tf_op jit(solution)/shard_map/ppermute | solution.py:61
  306.3 9.8 %collective-permute-start.38 = (bf16[2,64,1024]{2,1,0:T(8,128)(2,1)S(1)}, bf16[2,64,1024]{2,1,0:T(8,128)(2,1)S(1)}, u32[]{:S(2)}, u32[]{:S(2)}) collective-permute-start(bf16[2,64,1024]{2,1,0:T(8,128)(2,1)S(1)} %dynamic-slice_bitcast_fusion.8), channel_id=1, source_target_pairs={{0,8},{2,10},{4,12},{6,14},{8,0},{10,2},{12,4},{14,6},{16,24},{18,... | collective-permute-start | bytes 786440 | tf_op jit(solution)/shard_map/ppermute | solution.py:61
  316.2 15.5 %collective-permute-start.39 = (bf16[64,1024]{1,0:T(8,128)(2,1)S(1)}, bf16[64,1024]{1,0:T(8,128)(2,1)S(1)}, u32[]{:S(2)}, u32[]{:S(2)}) collective-permute-start(bf16[64,1024]{1,0:T(8,128)(2,1)S(1)} %dynamic-slice_bitcast_fusion.10), channel_id=1, source_target_pairs={{0,16},{2,18},{4,20},{6,22},{8,24},{10,26},{12,28},{14,30},{16,0},... | collective-permute-start | bytes 393224 | tf_op jit(solution)/shard_map/ppermute | solution.py:61
  338.5 11.2 %collective-permute-start.41 = (bf16[64,2048]{1,0:T(8,128)(2,1)S(1)}, bf16[64,2048]{1,0:T(8,128)(2,1)S(1)}, u32[]{:S(2)}, u32[]{:S(2)}) collective-permute-start(bf16[64,2048]{1,0:T(8,128)(2,1)S(1)} %bitcast.243), channel_id=1, source_target_pairs={{0,16},{2,18},{4,20},{6,22},{8,24},{10,26},{12,28},{14,30},{16,0},... | collective-permute-start | bytes 786440 | tf_op jit(solution)/shard_map/ppermute | solution.py:61
  349.7 15.3 %collective-permute-start.42 = (bf16[2,64,2048]{2,1,0:T(8,128)(2,1)S(1)}, bf16[2,64,2048]{2,1,0:T(8,128)(2,1)S(1)}, u32[]{:S(2)}, u32[]{:S(2)}) collective-permute-start(bf16[2,64,2048]{2,1,0:T(8,128)(2,1)S(1)} %maximum_select_fusion.13), channel_id=1, source_target_pairs={{0,8},{2,10},{4,12},{6,14},{8,0},{10,2},{12,4},{14,6},{16,24},{18,... | collective-permute-start | bytes 1572872 | tf_op jit(solution)/shard_map/ppermute | solution.py:61
  (92 other events, 492.4 us)
Sparse Core Ops, SparseCore 0:
  130.1 65.1 reduce-scatter.1
  209.2 139.0 all-gather.2
